TPU v7x, 128 devices: a whole 4x4x4 slice. The times are simulated.
128 devices in a mesh: gx: 4 (over z), gy: 4 (over y), gz: 8 (over x, core).
Axes of the slice: x: 4, y: 4, z: 4, core: 2. Of those that a mesh axis runs over, the one named last changes fastest.
Arguments:
- intensity: float32 [32, 128, 1024], P('gx', 'gy', 'gz'), may hold values from -24 to 24
- seed_labels: int32 [32, 128, 1024], P('gx', 'gy', 'gz'), may hold values from -1 to 7, as said below
Outputs:
- solution: float32 [8, 32, 128, 1024], P(None, 'gx', 'gy', 'gz')
- residual: float32 [8, 32, 128, 1024], P(None, 'gx', 'gy', 'gz')
- direction: float32 [8, 32, 128, 1024], P(None, 'gx', 'gy', 'gz')
Inputs may be any that keep to these rules, and one draw needn't show every extreme that they name: `seed_labels`: -1 marks an unseeded voxel, any other value is the voxel's seed label.
All inputs are finite; a program needn't handle non-finite values.
Results may differ from a plain program's by a relative error of at most 0.0003.
Values sent between devices are 32-bit elements; how exact they have to be, the bound alone decides.
No kernel may reach another device: no remote copies, remote signals or barrier semaphores. Data moves between devices by JAX's collectives and lax.ppermute only.
A program may use at most 128 MiB of HBM per device.

v0:
```python
import jax
import jax.numpy as jnp
from jax import lax
from jax.sharding import PartitionSpec as P

LABELS = 8
SWEEPS = 2
COARSE_SWEEPS = 6


BETA = 0.5
WFLOOR = 0.01
REACT = 0.01
PENALTY = 4.0
OMEGA = 0.8


def extended(shard, sides, width):
    for axis, dim in sides:
        size, length = (lax.axis_size(axis), shard.shape[dim])
        up = [(i, (i + 1) % size) for i in range(size - 1)]
        down = [(j, i) for i, j in up]
        last = lax.slice_in_dim(shard, length - width, length, axis=dim)
        leading = lax.slice_in_dim(shard, 0, width, axis=dim)
        before = lax.ppermute(last, axis, up)
        after = lax.ppermute(leading, axis, down)
        shard = jnp.concatenate([before, shard, after], axis=dim)
    return shard


def faces(vector):
    return extended(vector, (("gx", 1), ("gy", 2), ("gz", 3)), 1)


def label_sums(parts):
    return lax.psum(parts, ("gx", "gy", "gz"))


def edge_weight(contrast):
    return jnp.exp(-BETA * contrast * contrast) + WFLOOR


def make_level(uppers, lowers, source):
    diagonal = source + uppers[0] + uppers[1] + uppers[2] + lowers[0] + lowers[1] + lowers[2]
    return (uppers, lowers, source, diagonal)


def neighbour_sum(padded, grid_level):
    uppers, lowers = (grid_level[0], grid_level[1])
    summed = uppers[0] * padded[..., 2:, 1:-1, 1:-1] + lowers[0] * padded[..., :-2, 1:-1, 1:-1]
    summed = (
        summed + uppers[1] * padded[..., 1:-1, 2:, 1:-1] + lowers[1] * padded[..., 1:-1, :-2, 1:-1]
    )
    summed = (
        summed + uppers[2] * padded[..., 1:-1, 1:-1, 2:] + lowers[2] * padded[..., 1:-1, 1:-1, :-2]
    )
    return summed


def operate(vector, grid_level):
    return grid_level[3] * vector - neighbour_sum(faces(vector), grid_level)


def fold_x(weights, offset):
    extent = weights.shape
    return (
        weights[offset::2]
        .reshape(extent[0] // 2, extent[1] // 2, 2, extent[2] // 2, 2)
        .sum(axis=(2, 4))
    )


def fold_y(weights, offset):
    extent = weights.shape
    return (
        weights[:, offset::2]
        .reshape(extent[0] // 2, 2, extent[1] // 2, extent[2] // 2, 2)
        .sum(axis=(1, 4))
    )


def fold_z(weights, offset):
    extent = weights.shape
    return (
        weights[:, :, offset::2]
        .reshape(extent[0] // 2, 2, extent[1] // 2, 2, extent[2] // 2)
        .sum(axis=(1, 3))
    )


def block_sum(source):
    extent = source.shape
    return source.reshape(extent[0] // 2, 2, extent[1] // 2, 2, extent[2] // 2, 2).sum(
        axis=(1, 3, 5)
    )


def coarsen(grid_level):
    uppers, lowers, source = (grid_level[0], grid_level[1], grid_level[2])
    new_uppers = (fold_x(uppers[0], 1), fold_y(uppers[1], 1), fold_z(uppers[2], 1))
    new_lowers = (fold_x(lowers[0], 0), fold_y(lowers[1], 0), fold_z(lowers[2], 0))
    return make_level(new_uppers, new_lowers, block_sum(source))


def restrict(vector):
    extent = vector.shape
    return vector.reshape(extent[0], extent[1] // 2, 2, extent[2] // 2, 2, extent[3] // 2, 2).sum(
        axis=(2, 4, 6)
    )


def prolong(vector):
    extent = vector.shape
    spread = jnp.broadcast_to(
        vector[:, :, None, :, None, :, None], (extent[0], extent[1], 2, extent[2], 2, extent[3], 2)
    )
    return spread.reshape(extent[0], 2 * extent[1], 2 * extent[2], 2 * extent[3])


def smooth(approx, target, grid_level, apply_fn):
    return approx + OMEGA * (target - apply_fn(approx, grid_level)) / grid_level[3]


def plain_relax(target, grid_level):
    approx = OMEGA * target / grid_level[3]
    approx = smooth(approx, target, grid_level, operate)
    return (approx, target - operate(approx, grid_level))


def post_relax(approx, target, grid_level):
    for sweep_no in range(SWEEPS):
        approx = smooth(approx, target, grid_level, operate)
    return approx


def vcycle(target, levels, coarse_solve, pre_fn, post_fn):
    error_fine, left_fine = pre_fn(target, levels[0])
    target_mid = restrict(left_fine)
    error_mid, left_mid = pre_fn(target_mid, levels[1])
    target_low = restrict(left_mid)
    error_low = coarse_solve(target_low)
    error_mid = post_fn(error_mid + prolong(error_low), target_mid, levels[1])
    return post_fn(error_fine + prolong(error_mid), target, levels[0])


def label_dot(left, right):
    return jnp.sum(left * right, axis=(1, 2, 3))


def local(intensity, seed_labels):
    extent = intensity.shape
    padded = faces(intensity[None])[0]
    inner = padded[1:-1, 1:-1, 1:-1]
    pos_x = lax.broadcasted_iota(jnp.int32, extent, 0)
    pos_y = lax.broadcasted_iota(jnp.int32, extent, 1)
    pos_z = lax.broadcasted_iota(jnp.int32, extent, 2)
    top_x = (lax.axis_index("gx") == lax.axis_size("gx") - 1) & (pos_x == extent[0] - 1)
    top_y = (lax.axis_index("gy") == lax.axis_size("gy") - 1) & (pos_y == extent[1] - 1)
    top_z = (lax.axis_index("gz") == lax.axis_size("gz") - 1) & (pos_z == extent[2] - 1)
    bottom_x = (lax.axis_index("gx") == 0) & (pos_x == 0)
    bottom_y = (lax.axis_index("gy") == 0) & (pos_y == 0)
    bottom_z = (lax.axis_index("gz") == 0) & (pos_z == 0)
    upper_x = jnp.where(top_x, 0.0, edge_weight(padded[2:, 1:-1, 1:-1] - inner))
    upper_y = jnp.where(top_y, 0.0, edge_weight(padded[1:-1, 2:, 1:-1] - inner))
    upper_z = jnp.where(top_z, 0.0, edge_weight(padded[1:-1, 1:-1, 2:] - inner))
    lower_x = jnp.where(bottom_x, 0.0, edge_weight(inner - padded[:-2, 1:-1, 1:-1]))
    lower_y = jnp.where(bottom_y, 0.0, edge_weight(inner - padded[1:-1, :-2, 1:-1]))
    lower_z = jnp.where(bottom_z, 0.0, edge_weight(inner - padded[1:-1, 1:-1, :-2]))
    source = REACT + PENALTY * (seed_labels >= 0).astype(jnp.float32)
    label_axis = lax.broadcasted_iota(jnp.int32, (LABELS, 1, 1, 1), 0)
    right_side = PENALTY * (seed_labels[None] == label_axis).astype(jnp.float32)
    fine = make_level((upper_x, upper_y, upper_z), (lower_x, lower_y, lower_z), source)
    middle = coarsen(fine)
    coarse = coarsen(middle)

    def coarse_solve(target):
        approx = OMEGA * target / coarse[3]
        for sweep_no in range(COARSE_SWEEPS - 1):
            approx = smooth(approx, target, coarse, operate)
        return approx

    levels = (fine, middle)
    pre_fn, post_fn = (plain_relax, post_relax)
    precond = vcycle(right_side, levels, coarse_solve, pre_fn, post_fn)
    first_dot = label_sums(label_dot(right_side, precond))
    image = operate(precond, fine)
    curvature = label_sums(label_dot(precond, image))
    step_size = (first_dot / curvature)[:, None, None, None]
    solution = step_size * precond
    residual = right_side - step_size * image
    precond_next = vcycle(residual, levels, coarse_solve, pre_fn, post_fn)
    next_dot = label_sums(label_dot(residual, precond_next))
    direction = precond_next + (next_dot / first_dot)[:, None, None, None] * precond
    return (solution, residual, direction)


def solution(mesh):
    placed = (P("gx", "gy", "gz"), P("gx", "gy", "gz"))
    return jax.shard_map(
        local,
        mesh=mesh,
        in_specs=placed,
        out_specs=(P(None, "gx", "gy", "gz"), P(None, "gx", "gy", "gz"), P(None, "gx", "gy", "gz")),
        check_vma=False,
    )
```

profile of v0, /device:TPU:4, one launch (start us, length us, event | category | flops | bytes accessed | tf_op | source)
XLA Modules:
  0.0 1336.9 jit_solution(11426007766328284812)
XLA Ops:
  40.1 4.6 collective-permute-done.6
  46.1 4.5 collective-permute-start.9
  84.7 5.7 collective-permute-start.15
  124.2 10.6 reshape.139
  167.1 9.9 copy.2412
  176.9 13.1 reduce_sum.189
  292.2 5.2 collective-permute-start.33
  328.1 5.2 collective-permute-start.39
  364.0 5.2 collective-permute-start.45
  400.6 5.2 collective-permute-start.51
  435.8 5.2 collective-permute-start.57
  524.0 8.9 broadcast_in_dim.19
  533.0 10.7 copy.2484
  593.0 4.9 collective-permute-start.81
  629.0 4.9 collective-permute-start.87
  657.9 66.5 %all-reduce = (f32[8]{0:T(128)S(1)}, f32[8]{0:T(128)S(1)}) all-reduce(f32[8]{0:T(128)S(1)} %get-tuple-element.19, f32[8]{0:T(128)S(1)} %get-tuple-element.18), channel_id=1, replica_groups=mesh['gx'=4,'gy'=4,'gz'=8] {'gx','gy','gz'}, use_global_device_ids=true, to_apply=%region_17.18 | all-reduce | flops 16 | bytes 128 | tf_op jit(solution)/shard_map/psum | solution.py:36
  759.5 6.8 fusion.62
  777.9 4.9 collective-permute-start.99
  807.5 9.9 copy.2535
  817.4 13.1 reduce_sum.207
  917.1 5.2 collective-permute-start.117
  955.6 5.2 collective-permute-start.123
  994.1 5.4 collective-permute-start.129
  1032.8 5.2 collective-permute-start.135
  1071.3 5.2 collective-permute-start.141
  1165.6 8.9 broadcast_in_dim.21
  1174.5 10.6 copy.2589
  1219.0 6.5 fusion.33
  1236.0 4.9 collective-permute-start.165
  1258.4 7.5 multiply_reduce_fusion
  1265.9 65.7 %psum.23 = f32[8]{0:T(128)S(1)} all-reduce(f32[8]{0:T(128)S(1)} %get-tuple-element.22), channel_id=1, replica_groups=mesh['gx'=4,'gy'=4,'gz'=8] {'gx','gy','gz'}, use_global_device_ids=true, to_apply=%region_23.24 | all-reduce | flops 8 | bytes 64 | tf_op jit(solution)/shard_map/psum | solution.py:36
  1331.7 4.7 multiply_add_fusion
  (953 shorter events, 992.5 us)
Async XLA Ops:
  36.7 8.0 collective-permute-start.6
  82.8 56.0 %collective-permute-start.14 = (f32[8,10,1,128]{3,0,2,1:T(8,128)}, f32[8,10,1,128]{3,0,2,1:T(8,128)}, u32[]{:S(2)}, u32[]{:S(2)}) collective-permute-start(f32[8,10,1,128]{3,0,2,1:T(8,128)} %copy.2402), channel_id=1, source_target_pairs={{8,0},{16,8},{24,16},{9,1},{17,9},{25,17},{10,2},{18,10},{26,18},{... | collective-permute-start | bytes 122888 | tf_op jit(solution)/shard_map/ppermute | solution.py:26
  84.7 55.0 %collective-permute-start.15 = (f32[8,10,1,128]{3,0,2,1:T(8,128)}, f32[8,10,1,128]{3,0,2,1:T(8,128)}, u32[]{:S(2)}, u32[]{:S(2)}) collective-permute-start(f32[8,10,1,128]{3,0,2,1:T(8,128)} %copy.2404), channel_id=1, source_target_pairs={{0,8},{8,16},{16,24},{1,9},{9,17},{17,25},{2,10},{10,18},{18,26},{... | collective-permute-start | bytes 122888 | tf_op jit(solution)/shard_map/ppermute | solution.py:25
  150.0 10.2 collective-permute-start.17
  211.8 9.6 collective-permute-start.23
  231.9 25.8 %collective-permute-start.27 = (f32[8,6,1,64]{3,2,1,0:T(1,128)}, f32[8,6,1,64]{3,2,1,0:T(1,128)}, u32[]{:S(2)}, u32[]{:S(2)}) collective-permute-start(f32[8,6,1,64]{3,2,1,0:T(1,128)} %get-tuple-element.155), channel_id=1, source_target_pairs={{0,8},{8,16},{16,24},{1,9},{9,17},{17,25},{2,10},{10,18},{18,26},{... | collective-permute-start | bytes 36872 | tf_op jit(solution)/shard_map/ppermute | solution.py:25
  264.5 9.6 collective-permute-start.29
  290.8 8.5 collective-permute-start.32
  292.2 8.6 collective-permute-start.33
  326.9 8.4 collective-permute-start.38
  328.1 8.6 collective-permute-start.39
  362.8 8.4 collective-permute-start.44
  364.0 8.6 collective-permute-start.45
  399.4 8.4 collective-permute-start.50
  434.5 8.4 collective-permute-start.56
  435.8 8.0 collective-permute-start.57
  482.5 9.6 collective-permute-start.65
  511.8 9.6 collective-permute-start.71
  856.4 9.6 collective-permute-start.107
  886.9 9.6 collective-permute-start.113
  915.8 8.3 collective-permute-start.116
  917.1 8.6 collective-permute-start.117
  954.3 8.3 collective-permute-start.122
  955.6 8.6 collective-permute-start.123
  992.8 8.5 collective-permute-start.128
  994.1 8.8 collective-permute-start.129
  1031.5 8.3 collective-permute-start.134
  1032.8 8.6 collective-permute-start.135
  1070.0 8.3 collective-permute-start.140
  1071.3 8.6 collective-permute-start.141
  1123.0 9.6 collective-permute-start.149
  1151.8 9.6 collective-permute-start.155
  (263 other events, 7458.7 us)
where the time goes:
time: 1350 us; the launch traced here: 1340 us
  starting transfers between devices  386 us (29%)
  local copies, waits for them, and re-layouts  330 us (24%)
  waiting for transfers between devices  310 us (23%)
  other arithmetic  174 us (13%)
  blocking collectives  132 us (10%)
    ppermute x84, starting transfers between devices, extended(): before = lax.ppermute(last, axis, up)  255 us
    ppermute x84, waiting for transfers between devices, extended(): after = lax.ppermute(leading, axis, down)  190 us
    psum x2, blocking collectives, label_sums(): return lax.psum(parts, ('gx', 'gy', 'gz'))  132 us
    ppermute x84, starting transfers between devices, extended(): after = lax.ppermute(leading, axis, down)  130 us
    ppermute x84, waiting for transfers between devices, extended(): before = lax.ppermute(last, axis, up)  121 us
    slice x63, local copies, waits for them, and re-layouts, extended(): leading = lax.slice_in_dim(shard, 0, width, axis=dim)  51.1 us
    add x21, other arithmetic, smooth(): approx + OMEGA * (target - apply_fn(approx, grid_level)) / grid_level[3]  45.7 us
    unnamed x292, local copies, waits for them, and re-layouts  41.2 us
  transfers between devices with their start and end apart: 168, of which 127 were waited for; matrix products, arithmetic and copies ran while one was open for 11% of the time, Pallas kernels for 0%

commit v1 on v0

v1 whole, which is shorter than its diff:
```python
import functools

import jax
import jax.numpy as jnp
from jax import lax
from jax.experimental import pallas as pl
from jax.experimental.pallas import tpu as pltpu
from jax.sharding import PartitionSpec as P


LABELS = 8
BETA = 0.5
WFLOOR = 0.01
REACT = 0.01
PENALTY = 4.0
OMEGA = 0.8
KEEP = 1.0 - OMEGA
COARSE_SWEEPS = 6
VLIMIT = 40 * 1024 * 1024
F32 = jnp.float32


def lanes(v, shift):
    return pltpu.roll(v, shift % 128, 1)


def rows(v, shift):
    return pltpu.roll(v, shift % v.shape[0], 0)


def lane_id(shape):
    return lax.broadcasted_iota(jnp.int32, shape, 1)


def row_id(shape):
    return lax.broadcasted_iota(jnp.int32, shape, 0)


def neighbours(v_ref, uxs_ref, uy_ref, uz_ref, x, stride, ghost):
    if ghost:
        below, v, above = v_ref[x], v_ref[x + 1], v_ref[x + 2]
    else:
        last = v_ref.shape[0] - 1
        below, v, above = v_ref[jnp.maximum(x - 1, 0)], v_ref[x], v_ref[jnp.minimum(x + 1, last)]
    uy, uz = uy_ref[x], uz_ref[x]
    total = uxs_ref[x + 1] * above + uxs_ref[x] * below
    total = total + uy * lanes(v, -stride) + lanes(uy * v, stride)
    total = total + uz * rows(v, -1) + rows(uz * v, 1)
    return v, total


def diagonal(source, uxs_ref, uy_ref, uz_ref, x, stride):
    uy, uz = uy_ref[x], uz_ref[x]
    return source + uxs_ref[x + 1] + uxs_ref[x] + uy + lanes(uy, stride) + uz + rows(uz, 1)


def ghosts(v_ref, n):
    v_ref[0] = lanes(v_ref[n], 1)
    v_ref[n + 1] = lanes(v_ref[1], -1)


def halo_kernel(i_ref, s_ref, up_ref, dn_ref):
    lane = lane_id((32, 128))
    up = jnp.zeros((32, 128), F32)
    dn = jnp.zeros((32, 128), F32)
    for x in range(8):
        for side, v in ((0, i_ref[x]), (64, s_ref[x].astype(F32))):
            start = side + 8 * x
            here = (lane >= start) & (lane < start + 8)
            up = jnp.where(here, lanes(v, start - 120), up)
            dn = jnp.where(here, lanes(v, start), dn)
    up_ref[...] = up
    dn_ref[...] = dn


def pack_kernel(odd_ref, i_ref, s_ref, left_ref, right_ref, oi_ref, os_ref):
    odd = odd_ref[0]
    lane = lane_id((32, 128))
    low = lane < 64
    left, right = left_ref[...], right_ref[...]
    for which, (v_ref, o_ref) in enumerate(((i_ref, oi_ref), (s_ref, os_ref))):
        parts = ([], [])
        for x in range(4):
            a, b = v_ref[x].astype(F32), v_ref[x + 4].astype(F32)
            parts[0].append(jnp.where(low, a, lanes(b, 64)))
            parts[1].append(jnp.where(low, lanes(a, 64), b))
        from_left = left if which == 0 else lanes(left, 64)
        from_right = lanes(right, 64) if which == 0 else right
        own_above, own_below = from_left, from_right
        for x in range(8):
            v = v_ref[x].astype(F32)
            start = 64 + 8 * x
            own_above = jnp.where((lane >= start) & (lane < start + 8), lanes(v, start - 64), own_above)
            start = 8 * x
            own_below = jnp.where((lane >= start) & (lane < start + 8), lanes(v, start - 56), own_below)
        parts[0].append(own_above)
        parts[1].append(own_below)
        for label in range(LABELS):
            for half in range(2):
                slot = 2 * label + jnp.bitwise_xor(odd, half)
                for k in range(5):
                    o_ref[slot, k] = parts[half][k]


def assemble(r_ref, v_ref):
    for gx in range(4):
        for k in range(4):
            block = r_ref[4 * gx : 4 * gx + 4, k].reshape(128, 128)
            turned = block.T
            v_ref[8 * gx + k, 8:72] = turned[:64]
            v_ref[8 * gx + k + 4, 8:72] = turned[64:]
        turned = r_ref[4 * gx : 4 * gx + 4, 4].reshape(128, 128).T
        for x in range(8):
            v_ref[8 * gx + x, 0:8] = turned[8 * x : 8 * x + 8]
            v_ref[8 * gx + x, 72:80] = turned[64 + 8 * x : 72 + 8 * x]


def spread(v_ref, o_ref):
    for gx in range(4):
        for k in range(4):
            a, b = v_ref[8 * gx + k, 8:72], v_ref[8 * gx + k + 4, 8:72]
            o_ref[4 * gx : 4 * gx + 4, k] = jnp.concatenate([a, b], axis=0).T.reshape(4, 32, 128)


def plane_pair(v_ref, x, both_x, upper_z):
    total = v_ref[x, pl.ds(9, 32, stride=2), :]
    if not upper_z:
        total = total + v_ref[x, pl.ds(8, 32, stride=2), :]
    if both_x:
        total = total + plane_pair(v_ref, x + 1, False, upper_z)
    return total


def pack_pair(a, b):
    even = lane_id(a.shape) % 2 == 0
    return jnp.where(even, a + lanes(a, -1), b + lanes(b, 1))


def restrict_fine(v_ref, o_ref, slot):
    def body(x, c):
        a = plane_pair(v_ref, 2 * x, True, False)
        b = plane_pair(v_ref, 2 * x + 16, True, False)
        o_ref[slot, x] = pack_pair(a, b)
        return c

    lax.fori_loop(0, 8, body, 0)


def edge_weight(contrast):
    return jnp.exp(-BETA * contrast * contrast) + WFLOOR


def weights_kernel(zb_ref, r_ref, uxs_ref, uy_ref, uz_ref, w1_ref, v_ref):
    assemble(r_ref, v_ref)
    lane = lane_id((80, 128))
    place = row_id((80, 128)) + (zb_ref[0] - 8)
    cut = (place == -1) | (place == 1023)
    uxs_ref[0] = jnp.zeros((80, 128), F32)

    def body(x, c):
        v = v_ref[x]
        above = v_ref[jnp.minimum(x + 1, 31)]
        uxs_ref[x + 1] = jnp.where(x == 31, 0.0, edge_weight(above - v))
        uy_ref[x] = jnp.where(lane == 127, 0.0, edge_weight(lanes(v, -1) - v))
        uz_ref[x] = jnp.where(cut, 0.0, edge_weight(rows(v, -1) - v))
        return c

    lax.fori_loop(0, 32, body, 0)
    even = lane_id((32, 128)) % 2 == 0

    def coarse(x, c):
        w1_ref[0, x] = pack_pair(
            plane_pair(uxs_ref, 2 * x + 2, False, False), plane_pair(uxs_ref, 2 * x + 18, False, False)
        )
        a, b = plane_pair(uy_ref, 2 * x, True, False), plane_pair(uy_ref, 2 * x + 16, True, False)
        w1_ref[1, x] = jnp.where(even, lanes(a, -1), b)
        w1_ref[2, x] = pack_pair(
            plane_pair(uz_ref, 2 * x, True, True), plane_pair(uz_ref, 2 * x + 16, True, True)
        )
        return c

    lax.fori_loop(0, 8, coarse, 0)


def pre_relax(f_ref, g_ref, e_ref, t_ref, level, stride=1):
    uxs_ref, uy_ref, uz_ref, d_ref, di_ref = level

    def sweep(x, c):
        v, total = neighbours(g_ref, uxs_ref, uy_ref, uz_ref, x, 1, False)
        e_ref[x] = KEEP * v + di_ref[x] * (f_ref[x] + total)
        return c

    lax.fori_loop(0, 32, sweep, 0)

    def rest(x, c):
        v, total = neighbours(e_ref, uxs_ref, uy_ref, uz_ref, x, 1, False)
        t_ref[x] = f_ref[x] - d_ref[x] * v + total
        return c

    lax.fori_loop(0, 32, rest, 0)


def first_kernel(lab_ref, r_ref, uxs_ref, uy_ref, uz_ref, d_ref, di_ref, f_ref, e_ref, l1_ref, s_ref, g_ref):
    assemble(r_ref, s_ref)
    label = lab_ref[0].astype(F32)

    def setup(x, c):
        seed = s_ref[x]
        f = jnp.where(seed == label, PENALTY, 0.0)
        source = jnp.where(seed >= 0.0, REACT + PENALTY, REACT)
        d = diagonal(source, uxs_ref, uy_ref, uz_ref, x, 1)
        di = OMEGA / d
        s_ref[x] = source
        f_ref[x] = f
        d_ref[x] = d
        di_ref[x] = di
        g_ref[x] = di * f
        return c

    lax.fori_loop(0, 32, setup, 0)
    restrict_fine(s_ref, l1_ref, 1)
    pre_relax(f_ref, g_ref, e_ref, s_ref, (uxs_ref, uy_ref, uz_ref, d_ref, di_ref))
    restrict_fine(s_ref, l1_ref, 0)


def add_coarse(e_ref, c_ref, o_ref, p_ref):
    def body(x, c):
        v = c_ref[x]
        even = lane_id((40, 128)) % 2 == 0
        for part in range(2):
            if part == 0:
                w = jnp.where(even, v, 0.0)
                w = w + lanes(w, 1)
            else:
                w = jnp.where(even, 0.0, v)
                w = w + lanes(w, -1)
            p_ref[pl.ds(0, 40, stride=2), :] = w
            p_ref[pl.ds(1, 40, stride=2), :] = w
            wide = p_ref[...]
            at = 2 * x + 16 * part
            o_ref[at] = e_ref[at] + wide
            o_ref[at + 1] = e_ref[at + 1] + wide
        return c

    lax.fori_loop(0, 8, body, 0)


def post_relax(f_ref, a_ref, b_ref, level):
    uxs_ref, uy_ref, uz_ref, di_ref = level
    for src, dst in ((a_ref, b_ref), (b_ref, a_ref)):

        def sweep(x, c):
            v, total = neighbours(src, uxs_ref, uy_ref, uz_ref, x, 1, False)
            dst[x] = KEEP * v + di_ref[x] * (f_ref[x] + total)
            return c

        lax.fori_loop(0, 32, sweep, 0)


def dot_core(a_ref, b_ref):
    def body(x, c):
        p = a_ref[x, 8:72] * b_ref[x, 8:72]
        return c + p

    return jnp.sum(lax.fori_loop(0, 32, body, jnp.zeros((64, 128), F32)))


def middle_kernel(
    c_ref, uxs_ref, uy_ref, uz_ref, d_ref, di_ref, f_ref, e_ref,
    zo_ref, qo_ref, q_ref, e2_ref, l1_ref, dots_ref, a_ref, b_ref, p_ref,
):
    add_coarse(e_ref, c_ref, a_ref, p_ref)
    post_relax(f_ref, a_ref, b_ref, (uxs_ref, uy_ref, uz_ref, di_ref))

    def image(x, c):
        v, total = neighbours(a_ref, uxs_ref, uy_ref, uz_ref, x, 1, False)
        q = d_ref[x] * v - total
        q_ref[x] = q
        b_ref[x] = di_ref[x] * q
        return c

    lax.fori_loop(0, 32, image, 0)
    spread(a_ref, zo_ref)
    spread(q_ref, qo_ref)
    rz = dot_core(f_ref, a_ref)
    pq = dot_core(a_ref, q_ref)
    row = row_id((8, 128))
    dots_ref[...] = jnp.where(row == 0, rz, pq)
    pre_relax(q_ref, b_ref, e2_ref, a_ref, (uxs_ref, uy_ref, uz_ref, d_ref, di_ref))
    restrict_fine(a_ref, l1_ref, 0)


def last_kernel(
    c_ref, uxs_ref, uy_ref, uz_ref, di_ref, f_ref, q_ref, e_ref, dots_ref, wo_ref, t_ref, a_ref, b_ref, p_ref
):
    add_coarse(e_ref, c_ref, a_ref, p_ref)
    post_relax(q_ref, a_ref, b_ref, (uxs_ref, uy_ref, uz_ref, di_ref))
    spread(a_ref, wo_ref)
    fw = dot_core(f_ref, a_ref)
    qw = dot_core(q_ref, a_ref)
    lane = lane_id((1, 128))
    line = jnp.where(lane == 0, dots_ref[0:1, :], dots_ref[1:2, :])
    line = jnp.where(lane == 2, fw, jnp.where(lane == 3, qw, line))
    t_ref[...] = jnp.broadcast_to(line, (128, 128))


def frame1(o_ref, core, left, right, at):
    for x in range(8):
        o_ref[x + at, 0:24] = left(x)
        o_ref[x + at, 24:56] = core(x)
        o_ref[x + at, 56:80] = right(x)


def pair1(v_ref, x, both_x, upper_z):
    total = v_ref[x, pl.ds(1, 40, stride=2), :]
    if not upper_z:
        total = total + v_ref[x, pl.ds(0, 40, stride=2), :]
    if both_x:
        total = total + pair1(v_ref, x + 1, False, upper_z)
    return total


def coarse_kernel(
    w_ref, wl_ref, wr_ref, s_ref, sl_ref, sr_ref, f_ref, fl_ref, fr_ref, o_ref,
    ux1, uy1, uz1, f1, d1, di1, v1, v1b, t1, ux2, uy2, uz2, f2, di2, v2, v2b, p_ref,
):
    for k, (dst, at) in enumerate(((ux1, 1), (uy1, 0), (uz1, 0))):
        frame1(dst, lambda x: w_ref[k, x], lambda x: wl_ref[k, x], lambda x: wr_ref[k, x], at)
    frame1(f1, lambda x: f_ref[0, x], lambda x: fl_ref[0, x], lambda x: fr_ref[0, x], 0)
    frame1(t1, lambda x: s_ref[0, x], lambda x: sl_ref[0, x], lambda x: sr_ref[0, x], 0)
    ux1[0] = lanes(ux1[8], 1)

    valid = lane_id((40, 128)) % 4 < 2

    def fold(v):
        return jnp.where(valid, v, 0.0)

    for x in range(4):
        a = pair1(ux1, 2 * x + 2, False, False)
        ux2[x + 1] = fold(a + lanes(a, -2))
        uy2[x] = fold(lanes(pair1(uy1, 2 * x, True, False), -2))
        a = pair1(uz1, 2 * x, True, True)
        uz2[x] = fold(a + lanes(a, -2))
    ux2[0] = lanes(ux2[4], 1)
    for x in range(4):
        a = pair1(t1, 2 * x, True, False)
        d = diagonal(fold(a + lanes(a, -2)), ux2, uy2, uz2, x, 4)
        di2[x] = jnp.where(d > 0.0, OMEGA / d, 0.0)

    def setup(x, c):
        d = diagonal(t1[x], ux1, uy1, uz1, x, 2)
        di = jnp.where(d > 0.0, OMEGA / d, 0.0)
        d1[x] = d
        di1[x] = di
        v1[x + 1] = di * f1[x]
        return c

    lax.fori_loop(0, 8, setup, 0)

    def relax1(src, dst):
        ghosts(src, 8)

        def sweep(x, c):
            v, total = neighbours(src, ux1, uy1, uz1, x, 2, True)
            dst[x + 1] = KEEP * v + di1[x] * (f1[x] + total)
            return c

        lax.fori_loop(0, 8, sweep, 0)

    relax1(v1, v1b)
    ghosts(v1b, 8)

    def rest(x, c):
        v, total = neighbours(v1b, ux1, uy1, uz1, x, 2, True)
        t1[x] = f1[x] - d1[x] * v + total
        return c

    lax.fori_loop(0, 8, rest, 0)

    for x in range(4):
        a = pair1(t1, 2 * x, True, False)
        f2[x] = fold(a + lanes(a, -2))
        v2[x + 1] = di2[x] * f2[x]
    src, dst = v2, v2b
    for _ in range(COARSE_SWEEPS - 1):
        ghosts(src, 4)
        for x in range(4):
            v, total = neighbours(src, ux2, uy2, uz2, x, 4, True)
            dst[x + 1] = KEEP * v + di2[x] * (f2[x] + total)
        src, dst = dst, src

    for x in range(4):
        w = src[x + 1]
        w = w + lanes(w, 2)
        p_ref[pl.ds(0, 40, stride=2), :] = w
        p_ref[pl.ds(1, 40, stride=2), :] = w
        wide = p_ref[...]
        v1b[2 * x + 1] = v1b[2 * x + 1] + wide
        v1b[2 * x + 2] = v1b[2 * x + 2] + wide
    relax1(v1b, v1)
    relax1(v1, v1b)
    for x in range(8):
        o_ref[x] = v1b[x + 1, 20:60]


def output_kernel(odd_ref, sc_ref, seed_ref, z_ref, q_ref, w_ref, sol_ref, res_ref, dir_ref):
    label = pl.program_id(0)
    odd = odd_ref[0]
    step, beta = sc_ref[0, label], sc_ref[1, label]
    low = lane_id((32, 128)) < 64
    for x in range(4):
        pair = []
        for ref in (z_ref, q_ref, w_ref):
            a, b = ref[odd, x], ref[1 - odd, x]
            pair.append((jnp.where(low, a, lanes(b, 64)), jnp.where(low, lanes(a, 64), b)))
        for k in range(2):
            z, q, w = pair[0][k], pair[1][k], pair[2][k]
            at = x + 4 * k
            f = jnp.where(seed_ref[at] == label, PENALTY, 0.0)
            sol_ref[0, at] = step * z
            res_ref[0, at] = f - step * q
            dir_ref[0, at] = (1.0 + beta) * z - step * w


def sds(*shape):
    return jax.ShapeDtypeStruct(shape, F32)


def call(kernel, out, args, smem=0, scratch=(), cost=1000000, name=None):
    vmem, scalar = pl.BlockSpec(memory_space=pltpu.VMEM), pl.BlockSpec(memory_space=pltpu.SMEM)
    return pl.pallas_call(
        kernel,
        out_shape=out,
        in_specs=[scalar] * smem + [vmem] * (len(args) - smem),
        out_specs=jax.tree.map(lambda _: vmem, out),
        scratch_shapes=[pltpu.VMEM(s, F32) for s in scratch],
        compiler_params=pltpu.CompilerParams(vmem_limit_bytes=VLIMIT),
        cost_estimate=pl.CostEstimate(flops=cost, bytes_accessed=cost, transcendentals=0),
        name=name,
    )(*args)


FINE = (32, 80, 128)


def z_chain():
    def at(label, gz, half):
        return (2 * label + (half ^ (gz & 1))) * 8 + gz

    pairs = []
    for label in range(LABELS):
        for gz in range(8):
            pairs.append((at(label, gz, 0), at(label, gz, 1)))
            if gz < 7:
                pairs.append((at(label, gz, 1), at(label, gz + 1, 0)))
    return pairs


def swap_planes(v):
    every = ("gx", "gy", "gz")
    up = z_chain()
    down = [(b, a) for a, b in up]
    return lax.ppermute(v[:, :, 8:32], every, up), lax.ppermute(v[:, :, 0:24], every, down)


def local(intensity, seed_labels):
    gx, gy, gz = lax.axis_index("gx"), lax.axis_index("gy"), lax.axis_index("gz")
    group = ("gx", "gy")
    odd = (gz & 1).reshape(1)
    half = (gy ^ gz) & 1
    label = ((4 * gx + gy) // 2).reshape(1)
    z_base = (128 * gz + 64 * half).reshape(1)

    up, dn = call(halo_kernel, [sds(32, 128), sds(32, 128)], (intensity, seed_labels), name="halo")
    chain = [(i, i + 1) for i in range(7)]
    left = lax.ppermute(up, "gz", chain)
    right = lax.ppermute(dn, "gz", [(b, a) for a, b in chain])
    pi, ps = call(
        pack_kernel, [sds(16, 5, 32, 128)] * 2, (odd, intensity, seed_labels, left, right), smem=1, name="pack"
    )
    ri = lax.all_to_all(pi, group, 0, 0, tiled=True)
    rs = lax.all_to_all(ps, group, 0, 0, tiled=True)
    uxs, uy, uz, w1 = call(
        weights_kernel,
        [sds(33, 80, 128), sds(*FINE), sds(*FINE), sds(3, 8, 32, 128)],
        (z_base, ri),
        smem=1,
        scratch=[FINE],
        name="weights",
    )
    wl, wr = swap_planes(w1)
    d, di, f, e, l1 = call(
        first_kernel,
        [sds(*FINE)] * 4 + [sds(2, 8, 32, 128)],
        (label, rs, uxs, uy, uz),
        smem=1,
        scratch=[FINE, FINE],
        name="first",
    )
    ll, lr = swap_planes(l1)

    def coarse(f1, fl, fr):
        big, small = (8, 80, 128), (4, 40, 128)
        return call(
            coarse_kernel,
            [sds(8, 40, 128)],
            (w1, wl, wr, l1[1:2], ll[1:2], lr[1:2], f1, fl, fr),
            scratch=[(9, 80, 128), big, big, big, big, big, (10, 80, 128), (10, 80, 128), big]
            + [(5, 40, 128), small, small, small, small, (6, 40, 128), (6, 40, 128), (80, 128)],
            name="coarse",
        )[0]

    c1 = coarse(l1[0:1], ll[0:1], lr[0:1])
    zo, qo, q, e2, m1, dots = call(
        middle_kernel,
        [sds(16, 4, 32, 128)] * 2 + [sds(*FINE)] * 2 + [sds(1, 8, 32, 128), sds(8, 128)],
        (c1, uxs, uy, uz, d, di, f, e),
        scratch=[FINE, FINE, (80, 128)],
        name="middle",
    )
    ml, mr = swap_planes(m1)
    zr = lax.all_to_all(zo, group, 0, 0, tiled=True)
    qr = lax.all_to_all(qo, group, 0, 0, tiled=True)
    c2 = coarse(m1, ml, mr)
    wo, tiny = call(
        last_kernel,
        [sds(16, 4, 32, 128), sds(128, 128)],
        (c2, uxs, uy, uz, di, f, q, e2, dots),
        scratch=[FINE, FINE, (80, 128)],
        name="last",
    )
    sums = lax.all_to_all(tiny, ("gx", "gy", "gz"), 0, 0, tiled=True)
    wr_ = lax.all_to_all(wo, group, 0, 0, tiled=True)
    sums = sums.reshape(LABELS, 16, 128)[:, :, :4].sum(axis=1)
    rz, pq, fw, qw = sums[:, 0], sums[:, 1], sums[:, 2], sums[:, 3]
    step = rz / pq
    beta = step * (step * qw - fw) / rz
    scal = jnp.stack([step, beta])

    block = pl.BlockSpec((2, 4, 32, 128), lambda i: (i, 0, 0, 0))
    smem = pl.BlockSpec(memory_space=pltpu.SMEM)
    return tuple(
        pl.pallas_call(
            output_kernel,
            grid=(LABELS,),
            out_shape=[sds(8, 8, 32, 128)] * 3,
            in_specs=[smem, smem, pl.BlockSpec((8, 32, 128), lambda i: (0, 0, 0)), block, block, block],
            out_specs=[pl.BlockSpec((1, 8, 32, 128), lambda i: (i, 0, 0, 0))] * 3,
            compiler_params=pltpu.CompilerParams(vmem_limit_bytes=VLIMIT),
            name="output",
        )(odd, scal, seed_labels, zr, qr, wr_)
    )


def solution(mesh):
    placed = (P("gx", "gy", "gz"), P("gx", "gy", "gz"))
    return jax.shard_map(
        local,
        mesh=mesh,
        in_specs=placed,
        out_specs=(P(None, "gx", "gy", "gz"), P(None, "gx", "gy", "gz"), P(None, "gx", "gy", "gz")),
        check_vma=False,
    )
```

time: 1350 us -> 222 us (0.16)
  starting transfers between devices: 386 us -> 31.7 us
  local copies, waits for them, and re-layouts: 330 us -> 8.45 us
  waiting for transfers between devices: 310 us -> 32.4 us
  other arithmetic: 174 us -> 0.04 us
  Pallas kernels: 0 us -> 61.4 us
  blocking collectives: 132 us -> 84.6 us
    ppermute x168 -> x8, starting transfers between devices: 386 us -> 23.5 us  [the longest x3 12.2 us: swap_planes(): lax.ppermute(v[:, :, 8:32], every, up)]
    ppermute x168 -> x8, waiting for transfers between devices: 310 us -> 6.77 us  [the longest x3 3.82 us: swap_planes(): lax.ppermute(v[:, :, 0:24], every, down)]
    psum x2 -> x0, blocking collectives: 132 us -> none  [label_sums(): return lax.psum(parts, ('gx', 'gy', 'gz'))]
    slice x126 -> x7, local copies, waits for them, and re-layouts: 98.1 us -> 1.15 us  [the longest x3 0.89 us: swap_planes(): v[:, :, 0:24]]
    all_to_all x0 -> x4, blocking collectives: none -> 84.6 us  [the longest x1 30.2 us: local(): ri = lax.all_to_all(pi, group, 0, 0, tiled=True)]
    reduce_sum x20 -> x1, other arithmetic: 69.6 us -> 0.02 us  [local(): sums = sums.reshape(LABELS, 16, 128)[:, :, :4].sum(axis=1)]
    ppermute x56 -> x0, local copies, waits for them, and re-layouts: 69 us -> none  [the longest x28 34.6 us: extended(): before = lax.ppermute(last, axis, up)]
    pallas_call x0 -> x9, Pallas kernels: none -> 61.4 us  [the longest x8 57.1 us: call(): pl.pallas_call(kernel, out_shape=out, in_specs=[scalar] * smem + [vmem] *...]
  transfers between devices with their start and end apart: 168 -> 10, of which waited for: 127 -> 6; matrix products, arithmetic and copies ran while one was open for 11% -> 1% of each run, Pallas kernels for 0% -> 7%
where the time goes in v1:
time: 222 us; the launch traced here: 219 us
  blocking collectives  84.6 us (38%)
  Pallas kernels  61.4 us (28%)
  waiting for transfers between devices  32.4 us (15%)
  starting transfers between devices  31.7 us (14%)
  local copies, waits for them, and re-layouts  8.45 us (4%)
    pallas_call x8, Pallas kernels, call(): pl.pallas_call(kernel, out_shape=out, in_specs=[scalar] * smem + [vmem] *...  57.1 us
    all_to_all x1, blocking collectives, local(): ri = lax.all_to_all(pi, group, 0, 0, tiled=True)  30.2 us
    all_to_all x1, blocking collectives, local(): zr = lax.all_to_all(zo, group, 0, 0, tiled=True)  20.2 us
    all_to_all x1, blocking collectives, local(): qr = lax.all_to_all(qo, group, 0, 0, tiled=True)  19.5 us
    all_to_all x1, waiting for transfers between devices, local(): wr_ = lax.all_to_all(wo, group, 0, 0, tiled=True)  15.7 us
    all_to_all x1, blocking collectives, local(): sums = lax.all_to_all(tiny, ('gx', 'gy', 'gz'), 0, 0, tiled=True)  14.8 us
    ppermute x3, starting transfers between devices, swap_planes(): lax.ppermute(v[:, :, 8:32], every, up)  12.2 us
    all_to_all x1, waiting for transfers between devices, local(): rs = lax.all_to_all(ps, group, 0, 0, tiled=True)  9.88 us
  transfers between devices with their start and end apart: 10, of which 6 were waited for; matrix products, arithmetic and copies ran while one was open for 1% of the time, Pallas kernels for 7%

profile of v1, /device:TPU:4, one launch (start us, length us, event | category | flops | bytes accessed | tf_op | source)
XLA Modules:
  0.0 219.5 jit_solution(7438861423177018545)
XLA Ops:
  1.5 0.9 copy-done.8
  2.6 1.9 collective-permute-start
  4.6 3.6 %collective-permute-start.1 = (f32[32,128]{1,0:T(8,128)S(1)}, f32[32,128]{1,0:T(8,128)S(1)}, u32[]{:S(2)}, u32[]{:S(2)}) collective-permute-start(f32[32,128]{1,0:T(8,128)S(1)} %get-tuple-element.25), channel_id=1, source_target_pairs={{1,0},{2,1},{3,2},{4,3},{5,4},{6,5},{7,6},{9,8},{10,9},{11,10},{12... | collective-permute-start | bytes 49160 | tf_op jit(solution)/shard_map/ppermute | solution.py:477
  8.2 1.4 collective-permute-done.1.right_ref
  9.6 0.9 copy-done.5
  11.4 1.5 pack.1
  12.9 30.2 %all_to_all.34.r_ref = f32[16,5,32,128]{3,2,1,0:T(8,128)} all-to-all(f32[16,5,32,128]{3,2,1,0:T(8,128)S(1)} %get-tuple-element.26), channel_id=1, replica_groups=mesh['gx'=4,'gy'=4,'gz'=8] {'gx','gy'}, dimensions={0} | all-to-all | bytes 2621440 | tf_op jit(solution)/shard_map/all_to_all | solution.py:481
  43.1 4.4 %all-to-all-start.1 = ((f32[16,5,32,128]{3,2,1,0:T(8,128)}), f32[16,5,32,128]{3,2,1,0:T(8,128)}, u32[]{:S(2)}, u32[]{:S(2)}) async-start(f32[16,5,32,128]{3,2,1,0:T(8,128)} %get-tuple-element.28), calls=%async_computation.1 | async-start | bytes 2621440 | tf_op jit(solution)/shard_map/all_to_all | solution.py:482
  47.5 1.3 copy-done.3
  48.8 4.0 %weights.1 = (f32[33,80,128]{2,1,0:T(8,128)S(1)}, f32[32,80,128]{2,1,0:T(8,128)S(1)}, f32[32,80,128]{2,1,0:T(8,128)S(1)}, f32[3,8,32,128]{3,2,1,0:T(8,128)S(1)}) custom-call(s32[1]{0:T(128)} %bitcast.1.zb_ref, f32[16,5,32,128]{3,2,1,0:T(8,128)S(1)} %copy-done.3), custom_call_target="tpu_custom_call" | custom-call | flops 1000000 | bytes 1000000 | tf_op jit(solution)/shard_map/weights/pallas_call | solution.py:431
  52.8 1.0 copy-done
  54.7 1.9 collective-permute-start.3
  56.7 3.9 %collective-permute-start.2 = (f32[3,8,24,128]{3,2,1,0:T(8,128)}, f32[3,8,24,128]{3,2,1,0:T(8,128)}, u32[]{:S(2)}, u32[]{:S(2)}) collective-permute-start(f32[3,8,24,128]{3,2,1,0:T(8,128)} %get-tuple-element.50), channel_id=1, source_target_pairs={{0,8},{8,9},{9,1},{1,2},{2,10},{10,11},{11,3},{3,4},{4,12},{12,13}... | collective-permute-start | bytes 884744 | tf_op jit(solution)/shard_map/ppermute | solution.py:463
  60.6 9.9 %all-to-all-done.1.r_ref = f32[16,5,32,128]{3,2,1,0:T(8,128)} async-done(((f32[16,5,32,128]{3,2,1,0:T(8,128)}), f32[16,5,32,128]{3,2,1,0:T(8,128)}, u32[]{:S(2)}, u32[]{:S(2)}) %all-to-all-start.1) | async-done | bytes 1310752 | tf_op jit(solution)/shard_map/all_to_all | solution.py:482
  70.5 1.3 copy-done.1
  71.8 12.2 %first.1 = (f32[32,80,128]{2,1,0:T(8,128)S(1)}, f32[32,80,128]{2,1,0:T(8,128)S(1)}, f32[32,80,128]{2,1,0:T(8,128)S(1)}, f32[32,80,128]{2,1,0:T(8,128)S(1)}, f32[2,8,32,128]{3,2,1,0:T(8,128)S(1)}) custom-call(s32[1]{0:T(128)} %bitcast.2.lab_ref, f32[16,5,32,128]{3,2,1,0:T(8,128)} %all-to-all-done.1.r_ref, f32[33,80,128]{2,1,0:T(8,128)S(1)} %get-tuple-element.29.uxs_ref, ...), custom_call_target="tpu_custom_call" | custom-call | flops 1000000 | bytes 1000000 | tf_op jit(solution)/shard_map/first/pallas_call | solution.py:431
  84.0 1.9 collective-permute-start.5
  85.9 3.9 %collective-permute-start.4 = (f32[2,8,24,128]{3,2,1,0:T(8,128)S(1)}, f32[2,8,24,128]{3,2,1,0:T(8,128)S(1)}, u32[]{:S(2)}, u32[]{:S(2)}) collective-permute-start(f32[2,8,24,128]{3,2,1,0:T(8,128)S(1)} %get-tuple-element.54), channel_id=1, source_target_pairs={{0,8},{8,9},{9,1},{1,2},{2,10},{10,11},{11,3},{3,4},{4,12},{12,13}... | collective-permute-start | bytes 589832 | tf_op jit(solution)/shard_map/ppermute | solution.py:463
  89.9 3.2 %collective-permute-done.5 = f32[2,8,24,128]{3,2,1,0:T(8,128)S(1)} collective-permute-done((f32[2,8,24,128]{3,2,1,0:T(8,128)S(1)}, f32[2,8,24,128]{3,2,1,0:T(8,128)S(1)}, u32[]{:S(2)}, u32[]{:S(2)}) %collective-permute-start.5) | collective-permute-done | bytes 196640 | tf_op jit(solution)/shard_map/ppermute | solution.py:463
  93.1 6.3 %coarse.2.c_ref = f32[8,40,128]{2,1,0:T(8,128)S(1)} custom-call(f32[3,8,32,128]{3,2,1,0:T(8,128)S(1)} %get-tuple-element.27.w_ref, f32[3,8,24,128]{3,2,1,0:T(8,128)} %collective-permute-done.2.wl_ref, f32[3,8,24,128]{3,2,1,0:T(8,128)S(1)} %collective-permute-done.3.wr_ref, f32[1,8,32,128]{3,2,1,0:T(8,128)S(1)} %get-tuple-element.52.s_ref, ...), custom_call_target="tpu_custom_call" | custom-call | flops 1000000 | bytes 1000000 | tf_op jit(solution)/shard_map/coarse/pallas_call | solution.py:431
  99.4 18.5 %middle.1 = (f32[16,4,32,128]{3,2,1,0:T(8,128)S(1)}, f32[16,4,32,128]{3,2,1,0:T(8,128)S(1)}, f32[32,80,128]{2,1,0:T(8,128)S(1)}, f32[32,80,128]{2,1,0:T(8,128)S(...) custom-call(f32[8,40,128]{2,1,0:T(8,128)S(1)} %coarse.2.c_ref, f32[33,80,128]{2,1,0:T(8,128)S(1)} %get-tuple-element.29.uxs_ref, ...), custom_call_target="tpu_custom_call" | custom-call | flops 1000000 | bytes 1000000 | tf_op jit(solution)/shard_map/middle/pallas_call | solution.py:431
  117.9 1.9 collective-permute-start.7
  119.9 4.3 %collective-permute-start.6 = (f32[1,8,24,128]{3,2,1,0:T(8,128)S(1)}, f32[1,8,24,128]{3,2,1,0:T(8,128)S(1)}, u32[]{:S(2)}, u32[]{:S(2)}) collective-permute-start(f32[1,8,24,128]{3,2,1,0:T(8,128)S(1)} %get-tuple-element.60), channel_id=1, source_target_pairs={{0,8},{8,9},{9,1},{1,2},{2,10},{10,11},{11,3},{3,4},{4,12},{12,13}... | collective-permute-start | bytes 294920 | tf_op jit(solution)/shard_map/ppermute | solution.py:463
  124.8 1.5 collective-permute-done.6.fl_ref
  126.4 6.2 %coarse.3.c_ref = f32[8,40,128]{2,1,0:T(8,128)S(1)} custom-call(f32[3,8,32,128]{3,2,1,0:T(8,128)S(1)} %get-tuple-element.27.w_ref, f32[3,8,24,128]{3,2,1,0:T(8,128)} %collective-permute-done.2.wl_ref, f32[3,8,24,128]{3,2,1,0:T(8,128)S(1)} %collective-permute-done.3.wr_ref, f32[1,8,32,128]{3,2,1,0:T(8,128)S(1)} %get-tuple-element.52.s_ref, ...), custom_call_target="tpu_custom_call" | custom-call | flops 1000000 | bytes 1000000 | tf_op jit(solution)/shard_map/coarse/pallas_call | solution.py:431
  132.6 8.2 %last.1 = (f32[16,4,32,128]{3,2,1,0:T(8,128)S(1)}, f32[128,128]{1,0:T(8,128)S(1)}) custom-call(f32[8,40,128]{2,1,0:T(8,128)S(1)} %coarse.3.c_ref, f32[33,80,128]{2,1,0:T(8,128)S(1)} %get-tuple-element.29.uxs_ref, f32[32,80,128]{2,1,0:T(8,128)S(1)} %get-tuple-element.30.uy_ref, f32[32,80,128]{2,1,0:T(8,128)S(1)} %copy-done.2, ...), custom_call_target="tpu_custom_call" | custom-call | flops 1000000 | bytes 1000000 | tf_op jit(solution)/shard_map/last/pallas_call | solution.py:431
  140.9 14.8 %all_to_all.35 = f32[128,1,128]{2,1,0:T(1,128)S(1)} all-to-all(f32[128,1,128]{2,1,0:T(1,128)S(1)} %bitcast.26), channel_id=1, replica_groups=mesh['gx'=4,'gy'=4,'gz'=8] {'gx','gy','gz'}, dimensions={0} | all-to-all | bytes 131072 | tf_op jit(solution)/shard_map/all_to_all | solution.py:532
  155.7 20.2 %all_to_all.36.z_ref = f32[16,4,32,128]{3,2,1,0:T(8,128)S(1)} all-to-all(f32[16,4,32,128]{3,2,1,0:T(8,128)S(1)} %get-tuple-element.42), channel_id=1, replica_groups=mesh['gx'=4,'gy'=4,'gz'=8] {'gx','gy'}, dimensions={0} | all-to-all | bytes 2097152 | tf_op jit(solution)/shard_map/all_to_all | solution.py:522
  175.9 19.5 %all_to_all.37.q_ref = f32[16,4,32,128]{3,2,1,0:T(8,128)S(1)} all-to-all(f32[16,4,32,128]{3,2,1,0:T(8,128)S(1)} %get-tuple-element.43), channel_id=1, replica_groups=mesh['gx'=4,'gy'=4,'gz'=8] {'gx','gy'}, dimensions={0} | all-to-all | bytes 2097152 | tf_op jit(solution)/shard_map/all_to_all | solution.py:523
  195.3 3.8 %all-to-all-start.5 = ((f32[16,4,32,128]{3,2,1,0:T(8,128)}), f32[16,4,32,128]{3,2,1,0:T(8,128)S(1)}, u32[]{:S(2)}, u32[]{:S(2)}) async-start(f32[16,4,32,128]{3,2,1,0:T(8,128)} %copy-done.7), calls=%async_computation.5 | async-start | bytes 2097152 | tf_op jit(solution)/shard_map/all_to_all | solution.py:533
  199.4 15.7 %all-to-all-done.5.w_ref = f32[16,4,32,128]{3,2,1,0:T(8,128)S(1)} async-done(((f32[16,4,32,128]{3,2,1,0:T(8,128)}), f32[16,4,32,128]{3,2,1,0:T(8,128)S(1)}, u32[]{:S(2)}, u32[]{:S(2)}) %all-to-all-start.5) | async-done | bytes 1048608 | tf_op jit(solution)/shard_map/all_to_all | solution.py:533
  215.1 4.3 %output.1 = (f32[8,8,32,128]{3,2,1,0:T(8,128)}, f32[8,8,32,128]{3,2,1,0:T(8,128)}, f32[8,8,32,128]{3,2,1,0:T(8,128)}) custom-call(s32[1]{0:T(128)} %bitcast.odd_ref, f32[2,8]{1,0:T(2,128)S(1)} %pad_maximum_fusion.sc_ref, s32[8,32,128]{2,1,0:T(8,128)S(1)} %copy-done.6, f32[16,4,32,128]{3,2,1,0:T(8,128)S(1)} %all_to_all.36.z_ref, ...), custom_call_target="tpu_custom_call" | custom-call | tf_op jit(solution)/shard_map/output/pallas_call | solution.py:543
  (31 shorter events, 3.9 us)
Async XLA Ops:
  0.6 0.9 copy-start.4
  1.5 0.9 copy-start.8
  2.6 5.6 %collective-permute-start = (f32[32,128]{1,0:T(8,128)S(1)}, f32[32,128]{1,0:T(8,128)S(1)}, u32[]{:S(2)}, u32[]{:S(2)}) collective-permute-start(f32[32,128]{1,0:T(8,128)S(1)} %get-tuple-element.24), channel_id=1, source_target_pairs={{0,1},{1,2},{2,3},{3,4},{4,5},{5,6},{6,7},{8,9},{9,10},{10,11},{11... | collective-permute-start | bytes 49160 | tf_op jit(solution)/shard_map/ppermute | solution.py:476
  4.6 5.1 %collective-permute-start.1 = (f32[32,128]{1,0:T(8,128)S(1)}, f32[32,128]{1,0:T(8,128)S(1)}, u32[]{:S(2)}, u32[]{:S(2)}) collective-permute-start(f32[32,128]{1,0:T(8,128)S(1)} %get-tuple-element.25), channel_id=1, source_target_pairs={{1,0},{2,1},{3,2},{4,3},{5,4},{6,5},{7,6},{9,8},{10,9},{11,10},{12... | collective-permute-start | bytes 49160 | tf_op jit(solution)/shard_map/ppermute | solution.py:477
  9.6 0.9 copy-start.5
  10.5 0.9 copy-start.9
  43.1 27.4 %all-to-all-start.1 = ((f32[16,5,32,128]{3,2,1,0:T(8,128)}), f32[16,5,32,128]{3,2,1,0:T(8,128)}, u32[]{:S(2)}, u32[]{:S(2)}) async-start(f32[16,5,32,128]{3,2,1,0:T(8,128)} %get-tuple-element.28), calls=%async_computation.1 | async-start | bytes 2621440 | tf_op jit(solution)/shard_map/all_to_all | solution.py:482
  47.5 1.3 copy-start.3
  52.8 1.1 copy-start
  54.7 38.4 %collective-permute-start.3 = (f32[3,8,24,128]{3,2,1,0:T(8,128)}, f32[3,8,24,128]{3,2,1,0:T(8,128)S(1)}, u32[]{:S(2)}, u32[]{:S(2)}) collective-permute-start(f32[3,8,24,128]{3,2,1,0:T(8,128)} %get-tuple-element.49), channel_id=1, source_target_pairs={{8,0},{9,8},{1,9},{2,1},{10,2},{11,10},{3,11},{4,3},{12,4},{13,12}... | collective-permute-start | bytes 884744 | tf_op jit(solution)/shard_map/ppermute | solution.py:463
  56.7 36.5 %collective-permute-start.2 = (f32[3,8,24,128]{3,2,1,0:T(8,128)}, f32[3,8,24,128]{3,2,1,0:T(8,128)}, u32[]{:S(2)}, u32[]{:S(2)}) collective-permute-start(f32[3,8,24,128]{3,2,1,0:T(8,128)} %get-tuple-element.50), channel_id=1, source_target_pairs={{0,8},{8,9},{9,1},{1,2},{2,10},{10,11},{11,3},{3,4},{4,12},{12,13}... | collective-permute-start | bytes 884744 | tf_op jit(solution)/shard_map/ppermute | solution.py:463
  70.5 1.3 copy-start.1
  84.0 9.1 %collective-permute-start.5 = (f32[2,8,24,128]{3,2,1,0:T(8,128)S(1)}, f32[2,8,24,128]{3,2,1,0:T(8,128)S(1)}, u32[]{:S(2)}, u32[]{:S(2)}) collective-permute-start(f32[2,8,24,128]{3,2,1,0:T(8,128)S(1)} %get-tuple-element.53), channel_id=1, source_target_pairs={{8,0},{9,8},{1,9},{2,1},{10,2},{11,10},{3,11},{4,3},{12,4},{13,12}... | collective-permute-start | bytes 589832 | tf_op jit(solution)/shard_map/ppermute | solution.py:463
  85.9 7.2 %collective-permute-start.4 = (f32[2,8,24,128]{3,2,1,0:T(8,128)S(1)}, f32[2,8,24,128]{3,2,1,0:T(8,128)S(1)}, u32[]{:S(2)}, u32[]{:S(2)}) collective-permute-start(f32[2,8,24,128]{3,2,1,0:T(8,128)S(1)} %get-tuple-element.54), channel_id=1, source_target_pairs={{0,8},{8,9},{9,1},{1,2},{2,10},{10,11},{11,3},{3,4},{4,12},{12,13}... | collective-permute-start | bytes 589832 | tf_op jit(solution)/shard_map/ppermute | solution.py:463
  89.9 9.5 %copy-start.2 = (f32[32,80,128]{2,1,0:T(8,128)S(1)}, f32[32,80,128]{2,1,0:T(8,128)}, u32[]{:S(2)}) copy-start(f32[32,80,128]{2,1,0:T(8,128)} %copy-done) | copy-start | bytes 3932164
  117.9 6.9 %collective-permute-start.7 = (f32[1,8,24,128]{3,2,1,0:T(8,128)S(1)}, f32[1,8,24,128]{3,2,1,0:T(8,128)S(1)}, u32[]{:S(2)}, u32[]{:S(2)}) collective-permute-start(f32[1,8,24,128]{3,2,1,0:T(8,128)S(1)} %get-tuple-element.59), channel_id=1, source_target_pairs={{8,0},{9,8},{1,9},{2,1},{10,2},{11,10},{3,11},{4,3},{12,4},{13,12}... | collective-permute-start | bytes 294920 | tf_op jit(solution)/shard_map/ppermute | solution.py:463
  119.9 6.5 %collective-permute-start.6 = (f32[1,8,24,128]{3,2,1,0:T(8,128)S(1)}, f32[1,8,24,128]{3,2,1,0:T(8,128)S(1)}, u32[]{:S(2)}, u32[]{:S(2)}) collective-permute-start(f32[1,8,24,128]{3,2,1,0:T(8,128)S(1)} %get-tuple-element.60), channel_id=1, source_target_pairs={{0,8},{8,9},{9,1},{1,2},{2,10},{10,11},{11,3},{3,4},{4,12},{12,13}... | collective-permute-start | bytes 294920 | tf_op jit(solution)/shard_map/ppermute | solution.py:463
  140.9 54.5 %copy-start.7 = (f32[16,4,32,128]{3,2,1,0:T(8,128)}, f32[16,4,32,128]{3,2,1,0:T(8,128)S(1)}, u32[]{:S(2)}) copy-start(f32[16,4,32,128]{3,2,1,0:T(8,128)S(1)} %get-tuple-element.44) | copy-start | bytes 3145732
  195.3 19.8 %copy-start.6 = (s32[8,32,128]{2,1,0:T(8,128)S(1)}, s32[8,32,128]{2,1,0:T(8,128)}, u32[]{:S(2)}) copy-start(s32[8,32,128]{2,1,0:T(8,128)} %seed_ref.1) | copy-start | bytes 393220
  195.3 19.8 %all-to-all-start.5 = ((f32[16,4,32,128]{3,2,1,0:T(8,128)}), f32[16,4,32,128]{3,2,1,0:T(8,128)S(1)}, u32[]{:S(2)}, u32[]{:S(2)}) async-start(f32[16,4,32,128]{3,2,1,0:T(8,128)} %copy-done.7), calls=%async_computation.5 | async-start | bytes 2097152 | tf_op jit(solution)/shard_map/all_to_all | solution.py:533

commit v2 on v1

v2 whole, which is shorter than its diff:
```python
import functools

import jax
import jax.numpy as jnp
from jax import lax
from jax.experimental import pallas as pl
from jax.experimental.pallas import tpu as pltpu
from jax.sharding import PartitionSpec as P


LABELS = 8
BETA = 0.5
WFLOOR = 0.01
REACT = 0.01
PENALTY = 4.0
OMEGA = 0.8
KEEP = 1.0 - OMEGA
COARSE_SWEEPS = 6
VLIMIT = 44 * 1024 * 1024
F32 = jnp.float32


def lanes(v, shift):
    return pltpu.roll(v, shift % 128, 1)


def rows(v, shift):
    return pltpu.roll(v, shift % v.shape[0], 0)


def loop(n, body, group=8):
    def step(i, c):
        for k in range(group):
            body(group * i + k)
        return c

    if n == group:
        step(0, 0)
    else:
        lax.fori_loop(0, n // group, step, 0)


class Copies:
    def __init__(self, sems):
        self.sems, self.used, self.open = sems, 0, []

    def start(self, src, dst):
        copy = pltpu.make_async_copy(src, dst, self.sems.at[self.used])
        copy.start()
        self.used += 1
        self.open.append(copy)
        return copy

    def finish(self):
        for copy in self.open:
            copy.wait()
        self.open = []


def lane_id(shape):
    return lax.broadcasted_iota(jnp.int32, shape, 1)


def row_id(shape):
    return lax.broadcasted_iota(jnp.int32, shape, 0)


def neighbours(v_ref, uxs_ref, uy_ref, uz_ref, x, stride, ghost):
    if ghost:
        below, v, above = v_ref[x], v_ref[x + 1], v_ref[x + 2]
    else:
        last = v_ref.shape[0] - 1
        below, v, above = v_ref[jnp.maximum(x - 1, 0)], v_ref[x], v_ref[jnp.minimum(x + 1, last)]
    uy, uz = uy_ref[x], uz_ref[x]
    total = uxs_ref[x + 1] * above + uxs_ref[x] * below
    total = total + uy * lanes(v, -stride) + lanes(uy * v, stride)
    total = total + uz * rows(v, -1) + rows(uz * v, 1)
    return v, total


def diagonal(source, uxs_ref, uy_ref, uz_ref, x, stride):
    uy, uz = uy_ref[x], uz_ref[x]
    return source + uxs_ref[x + 1] + uxs_ref[x] + uy + lanes(uy, stride) + uz + rows(uz, 1)


def ghosts(v_ref, n):
    v_ref[0] = lanes(v_ref[n], 1)
    v_ref[n + 1] = lanes(v_ref[1], -1)


def pack_kernel(odd_ref, i_ref, s_ref, o_ref):
    odd = odd_ref[0]
    low = lane_id((32, 128)) < 64
    for field, v_ref in enumerate((i_ref, s_ref)):
        parts = ([], [])
        for x in range(4):
            a, b = v_ref[x].astype(F32), v_ref[x + 4].astype(F32)
            parts[0].append(jnp.where(low, a, lanes(b, 64)))
            parts[1].append(jnp.where(low, lanes(a, 64), b))
        for label in range(LABELS):
            for half in range(2):
                slot = 2 * label + jnp.bitwise_xor(odd, half)
                for k in range(4):
                    o_ref[slot, 4 * field + k] = parts[half][k]


def assemble_kernel(r_ref, core_ref, first_ref, last_ref):
    for gx in range(4):
        for k in range(8):
            turned = r_ref[4 * gx : 4 * gx + 4, k].reshape(128, 128).T
            for part in range(2):
                x = 32 * (k // 4) + 8 * gx + k % 4 + 4 * part
                core_ref[x] = turned[64 * part : 64 * part + 64]
                first_ref[x] = turned[64 * part : 64 * part + 8]
                last_ref[x] = turned[64 * part + 56 : 64 * part + 64]


def spread(v_ref, o_ref, field, copies, out_ref):
    for gx in range(4):
        for k in range(4):
            a, b = v_ref[8 * gx + k, 8:72], v_ref[8 * gx + k + 4, 8:72]
            turned = jnp.concatenate([a, b], axis=0).T.reshape(4, 32, 128)
            o_ref[4 * gx : 4 * gx + 4, 32 * (4 * field + k) : 32 * (4 * field + k + 1)] = turned
        part = (pl.ds(4 * gx, 4), pl.ds(128 * field, 128))
        copies.start(o_ref.at[part], out_ref.at[part])


def plane_pair(v_ref, x, both_x, upper_z):
    total = v_ref[x, pl.ds(9, 32, stride=2), :]
    if not upper_z:
        total = total + v_ref[x, pl.ds(8, 32, stride=2), :]
    if both_x:
        total = total + plane_pair(v_ref, x + 1, False, upper_z)
    return total


def pack_pair(a, b):
    even = lane_id(a.shape) % 2 == 0
    return jnp.where(even, a + lanes(a, -1), b + lanes(b, 1))


def restrict_fine(v_ref, o_ref, slot):
    def body(x):
        a = plane_pair(v_ref, 2 * x, True, False)
        b = plane_pair(v_ref, 2 * x + 16, True, False)
        o_ref[slot, x] = pack_pair(a, b)

    loop(8, body)


def edge_weight(contrast):
    return jnp.exp(-BETA * contrast * contrast) + WFLOOR


def pre_relax(f_ref, g_ref, e_ref, t_ref, level, then):
    uxs_ref, uy_ref, uz_ref, d_ref, di_ref = level

    def sweep(x):
        v, total = neighbours(g_ref, uxs_ref, uy_ref, uz_ref, x, 1, False)
        e_ref[x] = KEEP * v + di_ref[x] * (f_ref[x] + total)

    loop(32, sweep)
    then()

    def rest(x):
        v, total = neighbours(e_ref, uxs_ref, uy_ref, uz_ref, x, 1, False)
        t_ref[x] = f_ref[x] - d_ref[x] * v + total

    loop(32, rest)


def first_kernel(
    zb_ref, lab_ref, core_hbm, left_hbm, right_hbm,
    uxs_hbm, uy_hbm, uz_hbm, d_hbm, di_hbm, f_hbm, e_hbm, l1_ref,
    uxs_ref, uy_ref, uz_ref, d_ref, di_ref, f_ref, e_ref, v_ref, s_ref, sems,
):
    copies = Copies(sems)
    for base, dst in ((0, v_ref), (32, s_ref)):
        for src, at, n in ((left_hbm, 0, 8), (core_hbm, 8, 64), (right_hbm, 72, 8)):
            copies.start(src.at[pl.ds(base, 32)], dst.at[:, pl.ds(at, n)])
    arrived, copies.open = copies.open, []
    for copy in arrived[:3]:
        copy.wait()
    lane = lane_id((80, 128))
    place = row_id((80, 128)) + (zb_ref[0] - 8)
    cut = (place == -1) | (place == 1023)
    uxs_ref[0] = jnp.zeros((80, 128), F32)

    def body(x):
        v = v_ref[x]
        above = v_ref[jnp.minimum(x + 1, 31)]
        uxs_ref[x + 1] = jnp.where(x == 31, 0.0, edge_weight(above - v))
        uy_ref[x] = jnp.where(lane == 127, 0.0, edge_weight(lanes(v, -1) - v))
        uz_ref[x] = jnp.where(cut, 0.0, edge_weight(rows(v, -1) - v))

    loop(32, body, 4)
    even = lane_id((32, 128)) % 2 == 0

    def coarse(x):
        l1_ref[2, x] = pack_pair(
            plane_pair(uxs_ref, 2 * x + 2, False, False), plane_pair(uxs_ref, 2 * x + 18, False, False)
        )
        a, b = plane_pair(uy_ref, 2 * x, True, False), plane_pair(uy_ref, 2 * x + 16, True, False)
        l1_ref[3, x] = jnp.where(even, lanes(a, -1), b)
        l1_ref[4, x] = pack_pair(
            plane_pair(uz_ref, 2 * x, True, True), plane_pair(uz_ref, 2 * x + 16, True, True)
        )

    loop(8, coarse)
    copies.start(uxs_ref, uxs_hbm)
    copies.start(uy_ref, uy_hbm)
    copies.start(uz_ref, uz_hbm)
    for copy in arrived[3:]:
        copy.wait()
    label = lab_ref[0].astype(F32)

    def setup(x):
        seed = s_ref[x]
        f = jnp.where(seed == label, PENALTY, 0.0)
        source = jnp.where(seed >= 0.0, REACT + PENALTY, REACT)
        d = diagonal(source, uxs_ref, uy_ref, uz_ref, x, 1)
        di = OMEGA / d
        s_ref[x] = source
        f_ref[x] = f
        d_ref[x] = d
        di_ref[x] = di
        v_ref[x] = di * f

    loop(32, setup)
    copies.start(d_ref, d_hbm)
    copies.start(di_ref, di_hbm)
    copies.start(f_ref, f_hbm)
    restrict_fine(s_ref, l1_ref, 1)
    pre_relax(f_ref, v_ref, e_ref, s_ref, (uxs_ref, uy_ref, uz_ref, d_ref, di_ref), lambda: copies.start(e_ref, e_hbm))
    restrict_fine(s_ref, l1_ref, 0)
    copies.finish()


def add_coarse(e_ref, c_ref, o_ref, p_ref):
    even = lane_id((40, 128)) % 2 == 0

    def body(x):
        v = c_ref[x]
        for part in range(2):
            if part == 0:
                w = jnp.where(even, v, 0.0)
                w = w + lanes(w, 1)
            else:
                w = jnp.where(even, 0.0, v)
                w = w + lanes(w, -1)
            at = 2 * x + 16 * part
            slot = x % 4 + 4 * part
            p_ref[slot, pl.ds(0, 40, stride=2), :] = w
            p_ref[slot, pl.ds(1, 40, stride=2), :] = w
            wide = p_ref[slot]
            o_ref[at] = e_ref[at] + wide
            o_ref[at + 1] = e_ref[at + 1] + wide

    loop(8, body)


def post_relax(f_ref, a_ref, b_ref, level):
    uxs_ref, uy_ref, uz_ref, di_ref = level
    for src, dst in ((a_ref, b_ref), (b_ref, a_ref)):

        def sweep(x):
            v, total = neighbours(src, uxs_ref, uy_ref, uz_ref, x, 1, False)
            dst[x] = KEEP * v + di_ref[x] * (f_ref[x] + total)

        loop(32, sweep)


def dot_core(a_ref, b_ref, c_ref=None):
    def body(i, total):
        for k in range(4):
            b = b_ref[4 * i + k, 8:72]
            if c_ref is not None:
                b = b + c_ref[4 * i + k, 8:72]
            total = total + a_ref[4 * i + k, 8:72] * b
        return total

    return jnp.sum(lax.fori_loop(0, 8, body, jnp.zeros((64, 128), F32)))


def middle_kernel(
    l1, ll, lr, f1, fl, fr, uxs_hbm, uy_hbm, uz_hbm, d_hbm, di_hbm, f_hbm, e_hbm,
    zq_hbm, q_hbm, e2_hbm, m1_ref, dots_ref,
    uxs_ref, uy_ref, uz_ref, d_ref, di_ref, f_ref, e_ref, zq_ref, q_ref, a_ref, b_ref, p_ref, c_ref, *rest,
):
    copies = Copies(rest[-1])
    load1(copies, (l1, ll, lr), (f1, fl, fr), rest)
    small, copies.open = copies.open, []
    for src, dst in ((e_hbm, e_ref), (uxs_hbm, uxs_ref), (uy_hbm, uy_ref), (uz_hbm, uz_ref), (di_hbm, di_ref),
                     (f_hbm, f_ref), (d_hbm, d_ref)):
        copies.start(src, dst)
    for copy in small:
        copy.wait()
    coarse_solve(c_ref, *rest[:-1])
    copies.finish()
    add_coarse(e_ref, c_ref, a_ref, p_ref)
    post_relax(f_ref, a_ref, b_ref, (uxs_ref, uy_ref, uz_ref, di_ref))
    spread(a_ref, zq_ref, 0, copies, zq_hbm)

    def image(x):
        v, total = neighbours(a_ref, uxs_ref, uy_ref, uz_ref, x, 1, False)
        q = d_ref[x] * v - total
        q_ref[x] = q
        b_ref[x] = di_ref[x] * q

    loop(32, image)
    copies.start(q_ref, q_hbm)
    spread(q_ref, zq_ref, 1, copies, zq_hbm)
    rz = dot_core(f_ref, a_ref)
    pq = dot_core(a_ref, q_ref)
    pre_relax(
        q_ref, b_ref, e_ref, a_ref, (uxs_ref, uy_ref, uz_ref, d_ref, di_ref), lambda: copies.start(e_ref, e2_hbm)
    )
    restrict_fine(a_ref, m1_ref, 0)
    qw = dot_core(e_ref, q_ref, a_ref)
    lane = lane_id((8, 128))
    dots_ref[...] = jnp.where(lane == 0, rz, jnp.where(lane == 1, pq, jnp.where(lane == 2, qw, 0.0)))
    copies.finish()


def last_kernel(
    l1, ll, lr, f1, fl, fr, uxs_hbm, uy_hbm, uz_hbm, di_hbm, q_hbm, e_hbm, dots_ref,
    wo_hbm, line_ref,
    uxs_ref, uy_ref, uz_ref, di_ref, q_ref, e_ref, wo_ref, a_ref, b_ref, p_ref, c_ref, *rest,
):
    copies = Copies(rest[-1])
    load1(copies, (l1, ll, lr), (f1, fl, fr), rest)
    small, copies.open = copies.open, []
    for src, dst in ((e_hbm, e_ref), (uxs_hbm, uxs_ref), (uy_hbm, uy_ref), (uz_hbm, uz_ref), (di_hbm, di_ref),
                     (q_hbm, q_ref)):
        copies.start(src, dst)
    for copy in small:
        copy.wait()
    energy = coarse_solve(c_ref, *rest[:-1])
    line_ref[...] = dots_ref[...] + jnp.where(lane_id((8, 128)) == 2, energy, 0.0)
    copies.finish()
    add_coarse(e_ref, c_ref, a_ref, p_ref)
    post_relax(q_ref, a_ref, b_ref, (uxs_ref, uy_ref, uz_ref, di_ref))
    spread(a_ref, wo_ref, 0, copies, wo_hbm)
    copies.finish()


def load1(copies, weights, target, scratch):
    ux1, uy1, uz1, f1, t1 = scratch[0], scratch[1], scratch[2], scratch[3], scratch[8]
    for (core, left, right), field, dst, at in (
        (weights, 2, ux1, 1), (weights, 3, uy1, 0), (weights, 4, uz1, 0), (weights, 1, t1, 0), (target, 0, f1, 0),
    ):
        for src, low, n in ((left, 0, 24), (core, 24, 32), (right, 56, 24)):
            copies.start(src.at[field], dst.at[pl.ds(at, 8), pl.ds(low, n)])


def pair1(v_ref, x, both_x, upper_z):
    total = v_ref[x, pl.ds(1, 40, stride=2), :]
    if not upper_z:
        total = total + v_ref[x, pl.ds(0, 40, stride=2), :]
    if both_x:
        total = total + pair1(v_ref, x + 1, False, upper_z)
    return total


def coarse_solve(
    o_ref, ux1, uy1, uz1, f1, d1, di1, v1, v1b, t1, ux2, uy2, uz2, f2, di2, v2, v2b, p_ref
):
    ux1[0] = lanes(ux1[8], 1)

    valid = lane_id((40, 128)) % 4 < 2

    def fold(v):
        return jnp.where(valid, v, 0.0)

    for x in range(4):
        a = pair1(ux1, 2 * x + 2, False, False)
        ux2[x + 1] = fold(a + lanes(a, -2))
        uy2[x] = fold(lanes(pair1(uy1, 2 * x, True, False), -2))
        a = pair1(uz1, 2 * x, True, True)
        uz2[x] = fold(a + lanes(a, -2))
    ux2[0] = lanes(ux2[4], 1)
    for x in range(4):
        a = pair1(t1, 2 * x, True, False)
        d = diagonal(fold(a + lanes(a, -2)), ux2, uy2, uz2, x, 4)
        di2[x] = jnp.where(d > 0.0, OMEGA / d, 0.0)

    def setup(x):
        d = diagonal(t1[x], ux1, uy1, uz1, x, 2)
        di = jnp.where(d > 0.0, OMEGA / d, 0.0)
        d1[x] = d
        di1[x] = di
        v1[x + 1] = di * f1[x]

    loop(8, setup)

    def relax1(src, dst):
        ghosts(src, 8)

        def sweep(x):
            v, total = neighbours(src, ux1, uy1, uz1, x, 2, True)
            dst[x + 1] = KEEP * v + di1[x] * (f1[x] + total)

        loop(8, sweep)

    relax1(v1, v1b)
    ghosts(v1b, 8)

    dot = jnp.zeros((32, 128), F32)
    for x in range(8):
        v, total = neighbours(v1b, ux1, uy1, uz1, x, 2, True)
        f = f1[x]
        r = f - d1[x] * v + total
        t1[x] = r
        dot = dot + (v * (f + r))[24:56]

    for x in range(4):
        a = pair1(t1, 2 * x, True, False)
        f2[x] = fold(a + lanes(a, -2))
        v2[x + 1] = di2[x] * f2[x]
    src, dst = v2, v2b
    for _ in range(COARSE_SWEEPS - 1):
        ghosts(src, 4)
        for x in range(4):
            v, total = neighbours(src, ux2, uy2, uz2, x, 4, True)
            dst[x + 1] = KEEP * v + di2[x] * (f2[x] + total)
        src, dst = dst, src

    low = row_id((40, 128))
    own = (low >= 12) & (low < 28)
    dot2 = jnp.zeros((40, 128), F32)
    for x in range(4):
        dot2 = dot2 + jnp.where(own, src[x + 1] * f2[x], 0.0)
    energy = jnp.sum(dot) + jnp.sum(dot2)

    for x in range(4):
        w = src[x + 1]
        w = w + lanes(w, 2)
        p_ref[x, pl.ds(0, 40, stride=2), :] = w
        p_ref[x, pl.ds(1, 40, stride=2), :] = w
        wide = p_ref[x]
        v1b[2 * x + 1] = v1b[2 * x + 1] + wide
        v1b[2 * x + 2] = v1b[2 * x + 2] + wide
    relax1(v1b, v1)
    relax1(v1, v1b)
    for x in range(8):
        o_ref[x] = v1b[x + 1, 20:60]
    return energy


def output_kernel(odd_ref, seed_ref, zq_ref, w_ref, sol_ref, res_ref, dir_ref):
    label = pl.program_id(0)
    odd = odd_ref[0]
    sums = w_ref[0, 128:136, :] + w_ref[1, 128:136, :]
    rz, pq, qw = sums[0:1, 0:1], sums[0:1, 1:2], sums[0:1, 2:3]
    step = rz / pq
    more = (step * step * qw) / rz
    low = lane_id((32, 128)) < 64
    for x in range(4):
        pair = []
        for ref, at in ((zq_ref, x), (zq_ref, x + 4), (w_ref, x)):
            a, b = ref[odd, 32 * at : 32 * at + 32], ref[1 - odd, 32 * at : 32 * at + 32]
            pair.append((jnp.where(low, a, lanes(b, 64)), jnp.where(low, lanes(a, 64), b)))
        for k in range(2):
            z, q, w = pair[0][k], pair[1][k], pair[2][k]
            at = x + 4 * k
            f = jnp.where(seed_ref[at] == label, PENALTY, 0.0)
            sol_ref[0, at] = step * z
            res_ref[0, at] = f - step * q
            dir_ref[0, at] = more * z - step * w


def sds(*shape):
    return jax.ShapeDtypeStruct(shape, F32)


def call(kernel, out, args, smem=0, vmem=0, scratch=(), sems=0, cost=1000000, name=None):
    here, scalar = pl.BlockSpec(memory_space=pltpu.VMEM), pl.BlockSpec(memory_space=pltpu.SMEM)
    away = pl.BlockSpec(memory_space=pl.ANY)
    args = list(args)
    for k in range(smem, len(args) - vmem):
        if args[k].shape in (FINE, TALL):
            args[k] = pltpu.with_memory_space_constraint(args[k], pltpu.HBM)
    return pl.pallas_call(
        kernel,
        out_shape=[pltpu.HBM(shape, F32) if far else sds(*shape) for shape, far in out],
        in_specs=[scalar] * smem + [away] * (len(args) - smem - vmem) + [here] * vmem,
        out_specs=[pl.BlockSpec(memory_space=pltpu.HBM) if far else here for _, far in out],
        scratch_shapes=[pltpu.VMEM(s, F32) for s in scratch] + ([pltpu.SemaphoreType.DMA((sems,))] if sems else []),
        compiler_params=pltpu.CompilerParams(vmem_limit_bytes=VLIMIT),
        cost_estimate=pl.CostEstimate(flops=cost, bytes_accessed=cost, transcendentals=0),
        name=name,
    )(*args)


FINE = (32, 80, 128)
TALL = (33, 80, 128)
LEVEL1 = (8, 80, 128)
LEVEL2 = (4, 40, 128)
COARSE = (
    [(9, 80, 128)] + [LEVEL1] * 5 + [(10, 80, 128)] * 2 + [LEVEL1]
    + [(5, 40, 128)] + [LEVEL2] * 4 + [(6, 40, 128)] * 2 + [(4, 80, 128)]
)


def z_chain():
    def at(label, gz, half):
        return (2 * label + (half ^ (gz & 1))) * 8 + gz

    pairs = []
    for label in range(LABELS):
        for gz in range(8):
            pairs.append((at(label, gz, 0), at(label, gz, 1)))
            if gz < 7:
                pairs.append((at(label, gz, 1), at(label, gz + 1, 0)))
    return pairs


def swap(first, last):
    every = ("gx", "gy", "gz")
    up = z_chain()
    down = [(b, a) for a, b in up]
    return lax.ppermute(last, every, up), lax.ppermute(first, every, down)


def swap1(v):
    return swap(v[:, :, 0:24], v[:, :, 8:32])


def local(intensity, seed_labels):
    gx, gy, gz = lax.axis_index("gx"), lax.axis_index("gy"), lax.axis_index("gz")
    group = ("gx", "gy")
    odd = (gz & 1).reshape(1)
    half = (gy ^ gz) & 1
    label = ((4 * gx + gy) // 2).reshape(1)
    z_base = (128 * gz + 64 * half).reshape(1)

    sent = call(
        pack_kernel, [((16, 8, 32, 128), False)], (odd, intensity, seed_labels), smem=1, vmem=2, name="pack"
    )[0]
    got = lax.all_to_all(sent, group, 0, 0, tiled=True)
    core, first, last = call(
        assemble_kernel,
        [((64, 64, 128), False), ((64, 8, 128), False), ((64, 8, 128), False)],
        (got,),
        vmem=1,
        name="turn",
    )
    left, right = swap(first, last)
    uxs, uy, uz, d, di, f, e, l1 = call(
        first_kernel,
        [(TALL, True)] + [(FINE, True)] * 6 + [((5, 8, 32, 128), False)],
        (z_base, label, core, left, right),
        smem=2,
        scratch=[TALL] + [FINE] * 8,
        sems=13,
        name="first",
    )
    ll, lr = swap1(l1)
    zq, q, e2, m1, dots = call(
        middle_kernel,
        [((16, 256, 128), True), (FINE, True), (FINE, True), ((1, 8, 32, 128), False), ((8, 128), False)],
        (l1, ll, lr, l1, ll, lr, uxs, uy, uz, d, di, f, e),
        scratch=[TALL] + [FINE] * 6 + [(16, 256, 128)] + [FINE] * 3 + [(8, 80, 128), (8, 40, 128)] + COARSE,
        sems=32,
        name="middle",
    )
    ml, mr = swap1(m1)
    zq, ml, mr = lax.optimization_barrier((zq, ml, mr))
    zqr = lax.all_to_all(zq, group, 0, 0, tiled=True)
    wo, line = call(
        last_kernel,
        [((16, 136, 128), True), ((8, 128), False)],
        (l1, ll, lr, m1, ml, mr, uxs, uy, uz, di, q, e2, dots),
        vmem=1,
        scratch=[TALL] + [FINE] * 5 + [(16, 128, 128)] + [FINE] * 2 + [(8, 80, 128), (8, 40, 128)] + COARSE,
        sems=25,
        name="last",
    )
    sums = lax.psum(line, "gz")
    wo, zqr = lax.optimization_barrier((wo, zqr))
    wo = lax.dynamic_update_slice(wo, jnp.broadcast_to(sums, (16, 8, 128)), (0, 128, 0))
    wr_ = lax.all_to_all(wo, group, 0, 0, tiled=True)

    smem = pl.BlockSpec(memory_space=pltpu.SMEM)
    return tuple(
        pl.pallas_call(
            output_kernel,
            grid=(LABELS,),
            out_shape=[sds(8, 8, 32, 128)] * 3,
            in_specs=[
                smem,
                pl.BlockSpec((8, 32, 128), lambda i: (0, 0, 0)),
                pl.BlockSpec((2, 256, 128), lambda i: (i, 0, 0)),
                pl.BlockSpec((2, 136, 128), lambda i: (i, 0, 0)),
            ],
            out_specs=[pl.BlockSpec((1, 8, 32, 128), lambda i: (i, 0, 0, 0))] * 3,
            compiler_params=pltpu.CompilerParams(vmem_limit_bytes=VLIMIT),
            name="output",
        )(odd, seed_labels, zqr, wr_)
    )


def solution(mesh):
    placed = (P("gx", "gy", "gz"), P("gx", "gy", "gz"))
    return jax.shard_map(
        local,
        mesh=mesh,
        in_specs=placed,
        out_specs=(P(None, "gx", "gy", "gz"), P(None, "gx", "gy", "gz"), P(None, "gx", "gy", "gz")),
        check_vma=False,
    )
```

time: 222 us -> 155 us (0.70)
  Pallas kernels: 61.4 us -> 31 us
  blocking collectives: 84.6 us -> 68 us
  starting transfers between devices: 31.7 us -> 21 us
  waiting for transfers between devices: 32.4 us -> 28.2 us
  local copies, waits for them, and re-layouts: 8.45 us -> 5.09 us
    pallas_call x8 -> x5, Pallas kernels: 57.1 us -> 27.2 us  [call(): pl.pallas_call(kernel, out_shape=[pltpu.HBM(shape, F32) if far else sds(*...]
    all_to_all x4 -> x2, blocking collectives: 84.6 us -> 57.2 us  [the longest x1 36.2 us: local(): got = lax.all_to_all(sent, group, 0, 0, tiled=True)]
    all_to_all x2 -> x1, waiting for transfers between devices: 25.6 us -> 11 us  [local(): zqr = lax.all_to_all(zq, group, 0, 0, tiled=True)]
    psum x0 -> x1, blocking collectives: none -> 10.7 us  [local(): sums = lax.psum(line, 'gz')]
    ppermute x8 -> x6, waiting for transfers between devices: 6.77 us -> 17.2 us  [swap(): return (lax.ppermute(last, every, up), lax.ppermute(first, every, down))]
    ppermute x8 -> x6, starting transfers between devices: 23.5 us -> 17.2 us  [swap(): return (lax.ppermute(last, every, up), lax.ppermute(first, every, down))]
    all_to_all x2 -> x1, starting transfers between devices: 8.17 us -> 3.74 us  [local(): zqr = lax.all_to_all(zq, group, 0, 0, tiled=True)]
    unnamed x20 -> x14, local copies, waits for them, and re-layouts: 7.3 us -> 4.37 us
  transfers between devices with their start and end apart: 10 -> 7, of which waited for: 6 -> 6; matrix products, arithmetic and copies ran while one was open for 1% -> 0% of each run, Pallas kernels for 7% -> 5%
where the time goes in v2:
time: 155 us; the launch traced here: 154 us
  blocking collectives  68 us (44%)
  Pallas kernels  31 us (20%)
  waiting for transfers between devices  28.2 us (18%)
  starting transfers between devices  21 us (14%)
  local copies, waits for them, and re-layouts  5.09 us (3%)
    all_to_all x1, blocking collectives, local(): got = lax.all_to_all(sent, group, 0, 0, tiled=True)  36.2 us
    pallas_call x5, Pallas kernels, call(): pl.pallas_call(kernel, out_shape=[pltpu.HBM(shape, F32) if far else sds(*...  27.2 us
    all_to_all x1, blocking collectives, local(): wr_ = lax.all_to_all(wo, group, 0, 0, tiled=True)  21 us
    ppermute x6, starting transfers between devices, swap(): return (lax.ppermute(last, every, up), lax.ppermute(first, every, down))  17.2 us
    ppermute x6, waiting for transfers between devices, swap(): return (lax.ppermute(last, every, up), lax.ppermute(first, every, down))  17.2 us
    all_to_all x1, waiting for transfers between devices, local(): zqr = lax.all_to_all(zq, group, 0, 0, tiled=True)  11 us
    psum x1, blocking collectives, local(): sums = lax.psum(line, 'gz')  10.7 us
    unnamed x14, local copies, waits for them, and re-layouts  4.37 us
  transfers between devices with their start and end apart: 7, of which 6 were waited for; matrix products, arithmetic and copies ran while one was open for 0% of the time, Pallas kernels for 5%

profile of v2, /device:TPU:4, one launch (start us, length us, event | category | flops | bytes accessed | tf_op | source)
XLA Modules:
  0.0 154.1 jit_solution(7354668469147489940)
XLA Ops:
  0.6 0.0 copy-start.2
  0.6 0.9 copy-done.2
  1.5 0.9 copy-done.4
  2.4 0.2 pack.1
  2.7 36.2 %all_to_all.15.r_ref = f32[16,8,32,128]{3,2,1,0:T(8,128)S(1)} all-to-all(f32[16,8,32,128]{3,2,1,0:T(8,128)S(1)} %pack.1), channel_id=1, replica_groups=mesh['gx'=4,'gy'=4,'gz'=8] {'gx','gy'}, dimensions={0} | all-to-all | bytes 4194304 | tf_op jit(solution)/shard_map/all_to_all | solution.py:540
  38.9 0.6 turn.1
  39.5 2.5 %collective-permute-start = (f32[64,8,128]{2,1,0:T(8,128)S(1)}, f32[64,8,128]{2,1,0:T(8,128)S(1)}, u32[]{:S(2)}, u32[]{:S(2)}) collective-permute-start(f32[64,8,128]{2,1,0:T(8,128)S(1)} %get-tuple-element.27), channel_id=1, source_target_pairs={{0,8},{8,9},{9,1},{1,2},{2,10},{10,11},{11,3},{3,4},{4,12},{12,13}... | collective-permute-start | bytes 786440 | tf_op jit(solution)/shard_map/ppermute | solution.py:522
  42.0 3.1 %collective-permute-start.1 = (f32[64,8,128]{2,1,0:T(8,128)S(1)}, f32[64,8,128]{2,1,0:T(8,128)S(1)}, u32[]{:S(2)}, u32[]{:S(2)}) collective-permute-start(f32[64,8,128]{2,1,0:T(8,128)S(1)} %get-tuple-element.28), channel_id=1, source_target_pairs={{8,0},{9,8},{1,9},{2,1},{10,2},{11,10},{3,11},{4,3},{12,4},{13,12}... | collective-permute-start | bytes 786440 | tf_op jit(solution)/shard_map/ppermute | solution.py:522
  45.1 2.1 %collective-permute-done.left_hbm = f32[64,8,128]{2,1,0:T(8,128)S(1)} collective-permute-done((f32[64,8,128]{2,1,0:T(8,128)S(1)}, f32[64,8,128]{2,1,0:T(8,128)S(1)}, u32[]{:S(2)}, u32[]{:S(2)}) %collective-permute-start) | collective-permute-done | bytes 262176 | tf_op jit(solution)/shard_map/ppermute | solution.py:522
  47.2 3.1 %collective-permute-done.1.right_hbm = f32[64,8,128]{2,1,0:T(8,128)S(1)} collective-permute-done((f32[64,8,128]{2,1,0:T(8,128)S(1)}, f32[64,8,128]{2,1,0:T(8,128)S(1)}, u32[]{:S(2)}, u32[]{:S(2)}) %collective-permute-start.1) | collective-permute-done | bytes 262176 | tf_op jit(solution)/shard_map/ppermute | solution.py:522
  50.3 5.5 %first.1 = (f32[33,80,128]{2,1,0:T(8,128)}, f32[32,80,128]{2,1,0:T(8,128)}, f32[32,80,128]{2,1,0:T(8,128)}, f32[32,80,128]{2,1,0:T(8,128)}, f32[32,80,128]{2,1,0...) custom-call(s32[1]{0:T(128)} %bitcast.1.zb_ref, s32[1]{0:T(128)} %bitcast.2.lab_ref, ...), custom_call_target="tpu_custom_call" | custom-call | flops 1000000 | bytes 1000000 | tf_op jit(solution)/shard_map/first/pallas_call | solution.py:483
  55.8 0.1 fusion
  55.9 2.5 %collective-permute-start.3 = (f32[5,8,24,128]{3,2,1,0:T(8,128)S(1)}, f32[5,8,24,128]{3,2,1,0:T(8,128)S(1)}, u32[]{:S(2)}, u32[]{:S(2)}) collective-permute-start(f32[5,8,24,128]{3,2,1,0:T(8,128)S(1)} %get-tuple-element.49), channel_id=1, source_target_pairs={{8,0},{9,8},{1,9},{2,1},{10,2},{11,10},{3,11},{4,3},{12,4},{13,12}... | collective-permute-start | bytes 1474568 | tf_op jit(solution)/shard_map/ppermute | solution.py:522
  58.4 3.3 %collective-permute-start.2 = (f32[5,8,24,128]{3,2,1,0:T(8,128)S(1)}, f32[5,8,24,128]{3,2,1,0:T(8,128)S(1)}, u32[]{:S(2)}, u32[]{:S(2)}) collective-permute-start(f32[5,8,24,128]{3,2,1,0:T(8,128)S(1)} %get-tuple-element.50), channel_id=1, source_target_pairs={{0,8},{8,9},{9,1},{1,2},{2,10},{10,11},{11,3},{3,4},{4,12},{12,13}... | collective-permute-start | bytes 1474568 | tf_op jit(solution)/shard_map/ppermute | solution.py:522
  61.7 8.7 %collective-permute-done.3.lr.fr = f32[5,8,24,128]{3,2,1,0:T(8,128)S(1)} collective-permute-done((f32[5,8,24,128]{3,2,1,0:T(8,128)S(1)}, f32[5,8,24,128]{3,2,1,0:T(8,128)S(1)}, u32[]{:S(2)}, u32[]{:S(2)}) %collective-permute-start.3) | collective-permute-done | bytes 491552 | tf_op jit(solution)/shard_map/ppermute | solution.py:522
  70.4 13.0 %middle.1 = (f32[16,256,128]{2,1,0:T(8,128)}, f32[32,80,128]{2,1,0:T(8,128)}, f32[32,80,128]{2,1,0:T(8,128)}, f32[1,8,32,128]{3,2,1,0:T(8,128)S(1)}, f32[8,128]{1,0:T(8,128)S(1)}) custom-call(f32[5,8,32,128]{3,2,1,0:T(8,128)S(1)} %get-tuple-element.29.l1.f1, f32[5,8,24,128]{3,2,1,0:T(8,128)S(1)} %collective-permute-done.2.ll.fl, ...), custom_call_target="tpu_custom_call" | custom-call | flops 1000000 | bytes 1000000 | tf_op jit(solution)/shard_map/middle/pallas_call | solution.py:483
  83.5 3.3 %collective-permute-start.5 = (f32[1,8,24,128]{3,2,1,0:T(8,128)S(1)}, f32[1,8,24,128]{3,2,1,0:T(8,128)S(1)}, u32[]{:S(2)}, u32[]{:S(2)}) collective-permute-start(f32[1,8,24,128]{3,2,1,0:T(8,128)S(1)} %get-tuple-element.51), channel_id=1, source_target_pairs={{8,0},{9,8},{1,9},{2,1},{10,2},{11,10},{3,11},{4,3},{12,4},{13,12}... | collective-permute-start | bytes 294920 | tf_op jit(solution)/shard_map/ppermute | solution.py:522
  86.8 2.5 %collective-permute-start.4 = (f32[1,8,24,128]{3,2,1,0:T(8,128)S(1)}, f32[1,8,24,128]{3,2,1,0:T(8,128)S(1)}, u32[]{:S(2)}, u32[]{:S(2)}) collective-permute-start(f32[1,8,24,128]{3,2,1,0:T(8,128)S(1)} %get-tuple-element.52), channel_id=1, source_target_pairs={{0,8},{8,9},{9,1},{1,2},{2,10},{10,11},{11,3},{3,4},{4,12},{12,13}... | collective-permute-start | bytes 294920 | tf_op jit(solution)/shard_map/ppermute | solution.py:522
  89.3 0.7 collective-permute-done.5.fr
  90.0 2.7 %collective-permute-done.4.fl = f32[1,8,24,128]{3,2,1,0:T(8,128)S(1)} collective-permute-done((f32[1,8,24,128]{3,2,1,0:T(8,128)S(1)}, f32[1,8,24,128]{3,2,1,0:T(8,128)S(1)}, u32[]{:S(2)}, u32[]{:S(2)}) %collective-permute-start.4) | collective-permute-done | bytes 98336 | tf_op jit(solution)/shard_map/ppermute | solution.py:522
  92.7 0.6 copy-done.5
  93.4 3.7 %all-to-all-start.1 = ((f32[16,256,128]{2,1,0:T(8,128)}), f32[16,256,128]{2,1,0:T(8,128)S(1)}, u32[]{:S(2)}, u32[]{:S(2)}) async-start(f32[16,256,128]{2,1,0:T(8,128)} %get-tuple-element.45), calls=%async_computation.1 | async-start | bytes 4194304 | tf_op jit(solution)/shard_map/all_to_all | solution.py:569
  97.1 0.0 copy-start.1
  97.1 1.0 copy-done.1
  98.1 0.9 copy-done.6
  99.0 7.9 %last.1 = (f32[16,136,128]{2,1,0:T(8,128)}, f32[8,128]{1,0:T(8,128)S(1)}) custom-call(f32[5,8,32,128]{3,2,1,0:T(8,128)S(1)} %get-tuple-element.29.l1.f1, f32[5,8,24,128]{3,2,1,0:T(8,128)S(1)} %copy-done.1, f32[5,8,24,128]{3,2,1,0:T(8,128)S(1)} %collective-permute-done.3.lr.fr, f32[1,8,32,128]{3,2,1,0:T(8,128)S(1)} %get-tuple-element.37.f1, ...), custom_call_target="tpu_custom_call" | custom-call | flops 1000000 | bytes 1000000 | tf_op jit(solution)/shard_map/last/pallas_call | solution.py:483
  106.9 0.0 copy-start.3
  106.9 10.7 %psum.7 = f32[8,128]{1,0:T(8,128)S(1)} all-reduce(f32[8,128]{1,0:T(8,128)S(1)} %get-tuple-element.48), channel_id=1, replica_groups=mesh['gx'=4,'gy'=4,'gz'=8] {'gz'}, use_global_device_ids=true, to_apply=%region_0.1 | all-reduce | flops 1024 | bytes 8192 | tf_op jit(solution)/shard_map/psum | solution.py:579
  117.7 11.0 %all-to-all-done.1.zq_ref = f32[16,256,128]{2,1,0:T(8,128)S(1)} async-done(((f32[16,256,128]{2,1,0:T(8,128)}), f32[16,256,128]{2,1,0:T(8,128)S(1)}, u32[]{:S(2)}, u32[]{:S(2)}) %all-to-all-start.1) | async-done | bytes 2097184 | tf_op jit(solution)/shard_map/all_to_all | solution.py:569
  128.7 0.6 broadcast_dynamic-update-slice_fusion
  129.3 21.0 %all_to_all.16.w_ref = f32[16,136,128]{2,1,0:T(8,128)S(1)} all-to-all(f32[16,136,128]{2,1,0:T(8,128)} %broadcast_dynamic-update-slice_fusion), channel_id=1, replica_groups=mesh['gx'=4,'gy'=4,'gz'=8] {'gx','gy'}, dimensions={0} | all-to-all | bytes 2228224 | tf_op jit(solution)/shard_map/all_to_all | solution.py:582
  150.3 3.8 %output.1 = (f32[8,8,32,128]{3,2,1,0:T(8,128)}, f32[8,8,32,128]{3,2,1,0:T(8,128)}, f32[8,8,32,128]{3,2,1,0:T(8,128)}) custom-call(s32[1]{0:T(128)} %bitcast.odd_ref, s32[8,32,128]{2,1,0:T(8,128)S(1)} %copy-done.3, f32[16,256,128]{2,1,0:T(8,128)S(1)} %all-to-all-done.1.zq_ref, f32[16,136,128]{2,1,0:T(8,128)S(1)} %all_to_all.16.w_ref), custom_call_target="tpu_custom_call" | custom-call | tf_op jit(solution)/shard_map/output/pallas_call | solution.py:586
  (8 shorter events, 0.0 us)
Async XLA Ops:
  0.6 0.9 copy-start.2
  1.5 0.9 copy-start.4
  39.5 7.7 %collective-permute-start = (f32[64,8,128]{2,1,0:T(8,128)S(1)}, f32[64,8,128]{2,1,0:T(8,128)S(1)}, u32[]{:S(2)}, u32[]{:S(2)}) collective-permute-start(f32[64,8,128]{2,1,0:T(8,128)S(1)} %get-tuple-element.27), channel_id=1, source_target_pairs={{0,8},{8,9},{9,1},{1,2},{2,10},{10,11},{11,3},{3,4},{4,12},{12,13}... | collective-permute-start | bytes 786440 | tf_op jit(solution)/shard_map/ppermute | solution.py:522
  42.0 8.3 %collective-permute-start.1 = (f32[64,8,128]{2,1,0:T(8,128)S(1)}, f32[64,8,128]{2,1,0:T(8,128)S(1)}, u32[]{:S(2)}, u32[]{:S(2)}) collective-permute-start(f32[64,8,128]{2,1,0:T(8,128)S(1)} %get-tuple-element.28), channel_id=1, source_target_pairs={{8,0},{9,8},{1,9},{2,1},{10,2},{11,10},{3,11},{4,3},{12,4},{13,12}... | collective-permute-start | bytes 786440 | tf_op jit(solution)/shard_map/ppermute | solution.py:522
  55.9 14.6 %collective-permute-start.3 = (f32[5,8,24,128]{3,2,1,0:T(8,128)S(1)}, f32[5,8,24,128]{3,2,1,0:T(8,128)S(1)}, u32[]{:S(2)}, u32[]{:S(2)}) collective-permute-start(f32[5,8,24,128]{3,2,1,0:T(8,128)S(1)} %get-tuple-element.49), channel_id=1, source_target_pairs={{8,0},{9,8},{1,9},{2,1},{10,2},{11,10},{3,11},{4,3},{12,4},{13,12}... | collective-permute-start | bytes 1474568 | tf_op jit(solution)/shard_map/ppermute | solution.py:522
  58.4 12.0 %collective-permute-start.2 = (f32[5,8,24,128]{3,2,1,0:T(8,128)S(1)}, f32[5,8,24,128]{3,2,1,0:T(8,128)S(1)}, u32[]{:S(2)}, u32[]{:S(2)}) collective-permute-start(f32[5,8,24,128]{3,2,1,0:T(8,128)S(1)} %get-tuple-element.50), channel_id=1, source_target_pairs={{0,8},{8,9},{9,1},{1,2},{2,10},{10,11},{11,3},{3,4},{4,12},{12,13}... | collective-permute-start | bytes 1474568 | tf_op jit(solution)/shard_map/ppermute | solution.py:522
  70.4 13.0 %copy-start = (f32[5,8,24,128]{3,2,1,0:T(8,128)}, f32[5,8,24,128]{3,2,1,0:T(8,128)S(1)}, u32[]{:S(2)}) copy-start(f32[5,8,24,128]{3,2,1,0:T(8,128)S(1)} %collective-permute-done.2.ll.fl) | copy-start | bytes 1474564
  83.5 6.5 %collective-permute-start.5 = (f32[1,8,24,128]{3,2,1,0:T(8,128)S(1)}, f32[1,8,24,128]{3,2,1,0:T(8,128)S(1)}, u32[]{:S(2)}, u32[]{:S(2)}) collective-permute-start(f32[1,8,24,128]{3,2,1,0:T(8,128)S(1)} %get-tuple-element.51), channel_id=1, source_target_pairs={{8,0},{9,8},{1,9},{2,1},{10,2},{11,10},{3,11},{4,3},{12,4},{13,12}... | collective-permute-start | bytes 294920 | tf_op jit(solution)/shard_map/ppermute | solution.py:522
  86.8 5.9 %collective-permute-start.4 = (f32[1,8,24,128]{3,2,1,0:T(8,128)S(1)}, f32[1,8,24,128]{3,2,1,0:T(8,128)S(1)}, u32[]{:S(2)}, u32[]{:S(2)}) collective-permute-start(f32[1,8,24,128]{3,2,1,0:T(8,128)S(1)} %get-tuple-element.52), channel_id=1, source_target_pairs={{0,8},{8,9},{9,1},{1,2},{2,10},{10,11},{11,3},{3,4},{4,12},{12,13}... | collective-permute-start | bytes 294920 | tf_op jit(solution)/shard_map/ppermute | solution.py:522
  92.7 0.6 copy-start.5
  93.4 35.3 %all-to-all-start.1 = ((f32[16,256,128]{2,1,0:T(8,128)}), f32[16,256,128]{2,1,0:T(8,128)S(1)}, u32[]{:S(2)}, u32[]{:S(2)}) async-start(f32[16,256,128]{2,1,0:T(8,128)} %get-tuple-element.45), calls=%async_computation.1 | async-start | bytes 4194304 | tf_op jit(solution)/shard_map/all_to_all | solution.py:569
  97.1 1.0 copy-start.1
  98.1 0.9 copy-start.6
  106.9 43.4 %copy-start.3 = (s32[8,32,128]{2,1,0:T(8,128)S(1)}, s32[8,32,128]{2,1,0:T(8,128)}, u32[]{:S(2)}) copy-start(s32[8,32,128]{2,1,0:T(8,128)} %seed_ref.1) | copy-start | bytes 393220

commit v3 on v2

--- a/solution.py
+++ b/solution.py
@@ -28,13 +28,18 @@
     return pltpu.roll(v, shift % v.shape[0], 0)
 
 
-def loop(n, body, group=8):
+def loop(n, body, group=16, acc=None):
     def step(i, c):
-        for k in range(group):
-            body(group * i + k)
+        sums = {}
+        for k in range(min(group, n)):
+            for slot, v in enumerate(body(group * i + k) or ()):
+                if v is not None and acc is not None:
+                    sums[slot] = sums[slot] + v if slot in sums else v
+        for slot, v in sums.items():
+            acc[slot] += v
         return c
 
-    if n == group:
+    if n <= group:
         step(0, 0)
     else:
         lax.fori_loop(0, n // group, step, 0)
@@ -88,7 +93,11 @@
     v_ref[n + 1] = lanes(v_ref[1], -1)
 
 
-def pack_kernel(odd_ref, i_ref, s_ref, o_ref):
+def pack_kernel(odd_ref, i_hbm, s_hbm, o_ref, i_ref, s_ref, sems):
+    copies = Copies(sems)
+    copies.start(i_hbm, i_ref)
+    copies.start(s_hbm, s_ref)
+    copies.finish()
     odd = odd_ref[0]
     low = lane_id((32, 128)) < 64
     for field, v_ref in enumerate((i_ref, s_ref)):
@@ -152,7 +161,7 @@
     return jnp.exp(-BETA * contrast * contrast) + WFLOOR
 
 
-def pre_relax(f_ref, g_ref, e_ref, t_ref, level, then):
+def pre_relax(f_ref, g_ref, e_ref, t_ref, level, then, acc=None):
     uxs_ref, uy_ref, uz_ref, d_ref, di_ref = level
 
     def sweep(x):
@@ -164,9 +173,12 @@
 
     def rest(x):
         v, total = neighbours(e_ref, uxs_ref, uy_ref, uz_ref, x, 1, False)
-        t_ref[x] = f_ref[x] - d_ref[x] * v + total
-
-    loop(32, rest)
+        f = f_ref[x]
+        t = f - d_ref[x] * v + total
+        t_ref[x] = t
+        return (None, None, (v * (f + t))[8:72])
+
+    loop(32, rest, acc=acc)
 
 
 def first_kernel(
@@ -270,22 +282,10 @@
         loop(32, sweep)
 
 
-def dot_core(a_ref, b_ref, c_ref=None):
-    def body(i, total):
-        for k in range(4):
-            b = b_ref[4 * i + k, 8:72]
-            if c_ref is not None:
-                b = b + c_ref[4 * i + k, 8:72]
-            total = total + a_ref[4 * i + k, 8:72] * b
-        return total
-
-    return jnp.sum(lax.fori_loop(0, 8, body, jnp.zeros((64, 128), F32)))
-
-
 def middle_kernel(
     l1, ll, lr, f1, fl, fr, uxs_hbm, uy_hbm, uz_hbm, d_hbm, di_hbm, f_hbm, e_hbm,
     zq_hbm, q_hbm, e2_hbm, m1_ref, dots_ref,
-    uxs_ref, uy_ref, uz_ref, d_ref, di_ref, f_ref, e_ref, zq_ref, q_ref, a_ref, b_ref, p_ref, c_ref, *rest,
+    uxs_ref, uy_ref, uz_ref, d_ref, di_ref, f_ref, e_ref, zq_ref, q_ref, a_ref, b_ref, dots_acc, p_ref, c_ref, *rest,
 ):
     copies = Copies(rest[-1])
     load1(copies, (l1, ll, lr), (f1, fl, fr), rest)
@@ -306,24 +306,25 @@
         q = d_ref[x] * v - total
         q_ref[x] = q
         b_ref[x] = di_ref[x] * q
-
-    loop(32, image)
+        return (f_ref[x] * v)[8:72], (v * q)[8:72]
+
+    dots_acc[...] = jnp.zeros_like(dots_acc)
+    loop(32, image, acc=dots_acc)
     copies.start(q_ref, q_hbm)
     spread(q_ref, zq_ref, 1, copies, zq_hbm)
-    rz = dot_core(f_ref, a_ref)
-    pq = dot_core(a_ref, q_ref)
     pre_relax(
-        q_ref, b_ref, e_ref, a_ref, (uxs_ref, uy_ref, uz_ref, d_ref, di_ref), lambda: copies.start(e_ref, e2_hbm)
+        q_ref, b_ref, e_ref, a_ref, (uxs_ref, uy_ref, uz_ref, d_ref, di_ref),
+        lambda: copies.start(e_ref, e2_hbm), dots_acc,
     )
     restrict_fine(a_ref, m1_ref, 0)
-    qw = dot_core(e_ref, q_ref, a_ref)
+    rz, pq, qw = jnp.sum(dots_acc[0]), jnp.sum(dots_acc[1]), jnp.sum(dots_acc[2])
     lane = lane_id((8, 128))
     dots_ref[...] = jnp.where(lane == 0, rz, jnp.where(lane == 1, pq, jnp.where(lane == 2, qw, 0.0)))
     copies.finish()
 
 
 def last_kernel(
-    l1, ll, lr, f1, fl, fr, uxs_hbm, uy_hbm, uz_hbm, di_hbm, q_hbm, e_hbm, dots_ref,
+    lab_ref, l1, ll, lr, f1, fl, fr, uxs_hbm, uy_hbm, uz_hbm, di_hbm, q_hbm, e_hbm, dots_ref,
     wo_hbm, line_ref,
     uxs_ref, uy_ref, uz_ref, di_ref, q_ref, e_ref, wo_ref, a_ref, b_ref, p_ref, c_ref, *rest,
 ):
@@ -336,7 +337,8 @@
     for copy in small:
         copy.wait()
     energy = coarse_solve(c_ref, *rest[:-1])
-    line_ref[...] = dots_ref[...] + jnp.where(lane_id((8, 128)) == 2, energy, 0.0)
+    line = dots_ref[...] + jnp.where(lane_id((8, 128)) == 2, energy, 0.0)
+    line_ref[...] = jnp.where(row_id((8, 128)) == lab_ref[0], line, 0.0)
     copies.finish()
     add_coarse(e_ref, c_ref, a_ref, p_ref)
     post_relax(q_ref, a_ref, b_ref, (uxs_ref, uy_ref, uz_ref, di_ref))
@@ -447,26 +449,28 @@
     return energy
 
 
-def output_kernel(odd_ref, seed_ref, zq_ref, w_ref, sol_ref, res_ref, dir_ref):
-    label = pl.program_id(0)
+def output_kernel(odd_ref, seed_ref, sums_ref, zq_ref, w_ref, sol_ref, res_ref, dir_ref):
     odd = odd_ref[0]
-    sums = w_ref[0, 128:136, :] + w_ref[1, 128:136, :]
-    rz, pq, qw = sums[0:1, 0:1], sums[0:1, 1:2], sums[0:1, 2:3]
-    step = rz / pq
-    more = (step * step * qw) / rz
+    everyone = jnp.sum(sums_ref[...], axis=0)
     low = lane_id((32, 128)) < 64
-    for x in range(4):
-        pair = []
-        for ref, at in ((zq_ref, x), (zq_ref, x + 4), (w_ref, x)):
-            a, b = ref[odd, 32 * at : 32 * at + 32], ref[1 - odd, 32 * at : 32 * at + 32]
-            pair.append((jnp.where(low, a, lanes(b, 64)), jnp.where(low, lanes(a, 64), b)))
-        for k in range(2):
-            z, q, w = pair[0][k], pair[1][k], pair[2][k]
-            at = x + 4 * k
-            f = jnp.where(seed_ref[at] == label, PENALTY, 0.0)
-            sol_ref[0, at] = step * z
-            res_ref[0, at] = f - step * q
-            dir_ref[0, at] = more * z - step * w
+    for j in range(2):
+        label = 2 * pl.program_id(0) + j
+        sums = jnp.sum(jnp.where(row_id((8, 128)) == label, everyone, 0.0), axis=0, keepdims=True)
+        rz, pq, qw = sums[:, 0:1], sums[:, 1:2], sums[:, 2:3]
+        step = rz / pq
+        more = (step * step * qw) / rz
+        for x in range(4):
+            pair = []
+            for ref, at in ((zq_ref, x), (zq_ref, x + 4), (w_ref, x)):
+                a, b = ref[2 * j + odd, 32 * at : 32 * at + 32], ref[2 * j + 1 - odd, 32 * at : 32 * at + 32]
+                pair.append((jnp.where(low, a, lanes(b, 64)), jnp.where(low, lanes(a, 64), b)))
+            for k in range(2):
+                z, q, w = pair[0][k], pair[1][k], pair[2][k]
+                at = x + 4 * k
+                f = jnp.where(seed_ref[at] == label, PENALTY, 0.0)
+                sol_ref[j, at] = step * z
+                res_ref[j, at] = f - step * q
+                dir_ref[j, at] = more * z - step * w
 
 
 def sds(*shape):
@@ -478,14 +482,14 @@
     away = pl.BlockSpec(memory_space=pl.ANY)
     args = list(args)
     for k in range(smem, len(args) - vmem):
-        if args[k].shape in (FINE, TALL):
+        if args[k].shape in (FINE, TALL, (8, 32, 128)):
             args[k] = pltpu.with_memory_space_constraint(args[k], pltpu.HBM)
     return pl.pallas_call(
         kernel,
         out_shape=[pltpu.HBM(shape, F32) if far else sds(*shape) for shape, far in out],
         in_specs=[scalar] * smem + [away] * (len(args) - smem - vmem) + [here] * vmem,
         out_specs=[pl.BlockSpec(memory_space=pltpu.HBM) if far else here for _, far in out],
-        scratch_shapes=[pltpu.VMEM(s, F32) for s in scratch] + ([pltpu.SemaphoreType.DMA((sems,))] if sems else []),
+        scratch_shapes=[pltpu.VMEM(s, F32) if isinstance(s, tuple) else s for s in scratch] + ([pltpu.SemaphoreType.DMA((sems,))] if sems else []),
         compiler_params=pltpu.CompilerParams(vmem_limit_bytes=VLIMIT),
         cost_estimate=pl.CostEstimate(flops=cost, bytes_accessed=cost, transcendentals=0),
         name=name,
@@ -535,7 +539,8 @@
     z_base = (128 * gz + 64 * half).reshape(1)
 
     sent = call(
-        pack_kernel, [((16, 8, 32, 128), False)], (odd, intensity, seed_labels), smem=1, vmem=2, name="pack"
+        pack_kernel, [((16, 8, 32, 128), False)], (odd, intensity, seed_labels), smem=1,
+        scratch=[(8, 32, 128), pltpu.VMEM((8, 32, 128), jnp.int32)], sems=2, name="pack",
     )[0]
     got = lax.all_to_all(sent, group, 0, 0, tiled=True)
     core, first, last = call(
@@ -560,7 +565,7 @@
         middle_kernel,
         [((16, 256, 128), True), (FINE, True), (FINE, True), ((1, 8, 32, 128), False), ((8, 128), False)],
         (l1, ll, lr, l1, ll, lr, uxs, uy, uz, d, di, f, e),
-        scratch=[TALL] + [FINE] * 6 + [(16, 256, 128)] + [FINE] * 3 + [(8, 80, 128), (8, 40, 128)] + COARSE,
+        scratch=[TALL] + [FINE] * 6 + [(16, 256, 128)] + [FINE] * 3 + [(3, 64, 128), (8, 80, 128), (8, 40, 128)] + COARSE,
         sems=32,
         name="middle",
     )
@@ -570,7 +575,8 @@
     wo, line = call(
         last_kernel,
         [((16, 136, 128), True), ((8, 128), False)],
-        (l1, ll, lr, m1, ml, mr, uxs, uy, uz, di, q, e2, dots),
+        (label, l1, ll, lr, m1, ml, mr, uxs, uy, uz, di, q, e2, dots),
+        smem=1,
         vmem=1,
         scratch=[TALL] + [FINE] * 5 + [(16, 128, 128)] + [FINE] * 2 + [(8, 80, 128), (8, 40, 128)] + COARSE,
         sems=25,
@@ -581,22 +587,22 @@
     wo = lax.dynamic_update_slice(wo, jnp.broadcast_to(sums, (16, 8, 128)), (0, 128, 0))
     wr_ = lax.all_to_all(wo, group, 0, 0, tiled=True)
 
-    smem = pl.BlockSpec(memory_space=pltpu.SMEM)
     return tuple(
         pl.pallas_call(
             output_kernel,
-            grid=(LABELS,),
+            grid=(LABELS // 2,),
             out_shape=[sds(8, 8, 32, 128)] * 3,
             in_specs=[
-                smem,
+                pl.BlockSpec(memory_space=pltpu.SMEM),
                 pl.BlockSpec((8, 32, 128), lambda i: (0, 0, 0)),
-                pl.BlockSpec((2, 256, 128), lambda i: (i, 0, 0)),
-                pl.BlockSpec((2, 136, 128), lambda i: (i, 0, 0)),
+                pl.BlockSpec((16, 8, 128), lambda i: (0, 16, 0)),
+                pl.BlockSpec((4, 256, 128), lambda i: (i, 0, 0)),
+                pl.BlockSpec((4, 136, 128), lambda i: (i, 0, 0)),
             ],
-            out_specs=[pl.BlockSpec((1, 8, 32, 128), lambda i: (i, 0, 0, 0))] * 3,
+            out_specs=[pl.BlockSpec((2, 8, 32, 128), lambda i: (i, 0, 0, 0))] * 3,
             compiler_params=pltpu.CompilerParams(vmem_limit_bytes=VLIMIT),
             name="output",
-        )(odd, seed_labels, zqr, wr_)
+        )(odd, seed_labels, wr_, zqr, wr_)
     )
 
 

time: 155 us -> 152 us (0.981)
  local copies, waits for them, and re-layouts: 5.09 us -> 3.29 us
    unnamed x14 -> x10, local copies, waits for them, and re-layouts: 4.37 us -> 2.57 us
where the time goes in v3:
time: 152 us; the launch traced here: 151 us
  blocking collectives  68 us (45%)
  Pallas kernels  29.6 us (19%)
  waiting for transfers between devices  28.2 us (19%)
  starting transfers between devices  21.2 us (14%)
  local copies, waits for them, and re-layouts  3.29 us (2%)
    all_to_all x1, blocking collectives, local(): got = lax.all_to_all(sent, group, 0, 0, tiled=True)  36.2 us
    pallas_call x5, Pallas kernels, call(): pl.pallas_call(kernel, out_shape=[pltpu.HBM(shape, F32) if far else sds(*...  27 us
    all_to_all x1, blocking collectives, local(): wr_ = lax.all_to_all(wo, group, 0, 0, tiled=True)  21 us
    ppermute x6, starting transfers between devices, swap(): return (lax.ppermute(last, every, up), lax.ppermute(first, every, down))  17.2 us
    ppermute x6, waiting for transfers between devices, swap(): return (lax.ppermute(last, every, up), lax.ppermute(first, every, down))  17.2 us
    all_to_all x1, waiting for transfers between devices, local(): zqr = lax.all_to_all(zq, group, 0, 0, tiled=True)  11 us
    psum x1, blocking collectives, local(): sums = lax.psum(line, 'gz')  10.7 us
    all_to_all x1, starting transfers between devices, local(): zqr = lax.all_to_all(zq, group, 0, 0, tiled=True)  3.91 us
  transfers between devices with their start and end apart: 7, of which 6 were waited for; matrix products, arithmetic and copies ran while one was open for 0% of the time, Pallas kernels for 5%

profile of v3, /device:TPU:4, one launch (start us, length us, event | category | flops | bytes accessed | tf_op | source)
XLA Modules:
  0.0 151.0 jit_solution(1353729518115267087)
XLA Ops:
  0.6 1.2 pack.1
  1.9 36.2 %all_to_all.15.r_ref = f32[16,8,32,128]{3,2,1,0:T(8,128)S(1)} all-to-all(f32[16,8,32,128]{3,2,1,0:T(8,128)S(1)} %pack.1), channel_id=1, replica_groups=mesh['gx'=4,'gy'=4,'gz'=8] {'gx','gy'}, dimensions={0} | all-to-all | bytes 4194304 | tf_op jit(solution)/shard_map/all_to_all | solution.py:545
  38.1 0.6 turn.1
  38.7 2.5 %collective-permute-start = (f32[64,8,128]{2,1,0:T(8,128)S(1)}, f32[64,8,128]{2,1,0:T(8,128)S(1)}, u32[]{:S(2)}, u32[]{:S(2)}) collective-permute-start(f32[64,8,128]{2,1,0:T(8,128)S(1)} %get-tuple-element.27), channel_id=1, source_target_pairs={{0,8},{8,9},{9,1},{1,2},{2,10},{10,11},{11,3},{3,4},{4,12},{12,13}... | collective-permute-start | bytes 786440 | tf_op jit(solution)/shard_map/ppermute | solution.py:526
  41.2 3.1 %collective-permute-start.1 = (f32[64,8,128]{2,1,0:T(8,128)S(1)}, f32[64,8,128]{2,1,0:T(8,128)S(1)}, u32[]{:S(2)}, u32[]{:S(2)}) collective-permute-start(f32[64,8,128]{2,1,0:T(8,128)S(1)} %get-tuple-element.28), channel_id=1, source_target_pairs={{8,0},{9,8},{1,9},{2,1},{10,2},{11,10},{3,11},{4,3},{12,4},{13,12}... | collective-permute-start | bytes 786440 | tf_op jit(solution)/shard_map/ppermute | solution.py:526
  44.3 2.1 %collective-permute-done.left_hbm = f32[64,8,128]{2,1,0:T(8,128)S(1)} collective-permute-done((f32[64,8,128]{2,1,0:T(8,128)S(1)}, f32[64,8,128]{2,1,0:T(8,128)S(1)}, u32[]{:S(2)}, u32[]{:S(2)}) %collective-permute-start) | collective-permute-done | bytes 262176 | tf_op jit(solution)/shard_map/ppermute | solution.py:526
  46.4 3.1 %collective-permute-done.1.right_hbm = f32[64,8,128]{2,1,0:T(8,128)S(1)} collective-permute-done((f32[64,8,128]{2,1,0:T(8,128)S(1)}, f32[64,8,128]{2,1,0:T(8,128)S(1)}, u32[]{:S(2)}, u32[]{:S(2)}) %collective-permute-start.1) | collective-permute-done | bytes 262176 | tf_op jit(solution)/shard_map/ppermute | solution.py:526
  49.5 5.4 %first.1 = (f32[33,80,128]{2,1,0:T(8,128)}, f32[32,80,128]{2,1,0:T(8,128)}, f32[32,80,128]{2,1,0:T(8,128)}, f32[32,80,128]{2,1,0:T(8,128)}, f32[32,80,128]{2,1,0...) custom-call(s32[1]{0:T(128)} %bitcast.2.zb_ref, s32[1]{0:T(128)} %bitcast.1.lab_ref, ...), custom_call_target="tpu_custom_call" | custom-call | flops 1000000 | bytes 1000000 | tf_op jit(solution)/shard_map/first/pallas_call | solution.py:487
  54.9 0.1 fusion
  54.9 2.5 %collective-permute-start.3 = (f32[5,8,24,128]{3,2,1,0:T(8,128)S(1)}, f32[5,8,24,128]{3,2,1,0:T(8,128)S(1)}, u32[]{:S(2)}, u32[]{:S(2)}) collective-permute-start(f32[5,8,24,128]{3,2,1,0:T(8,128)S(1)} %get-tuple-element.49), channel_id=1, source_target_pairs={{8,0},{9,8},{1,9},{2,1},{10,2},{11,10},{3,11},{4,3},{12,4},{13,12}... | collective-permute-start | bytes 1474568 | tf_op jit(solution)/shard_map/ppermute | solution.py:526
  57.5 3.3 %collective-permute-start.2 = (f32[5,8,24,128]{3,2,1,0:T(8,128)S(1)}, f32[5,8,24,128]{3,2,1,0:T(8,128)S(1)}, u32[]{:S(2)}, u32[]{:S(2)}) collective-permute-start(f32[5,8,24,128]{3,2,1,0:T(8,128)S(1)} %get-tuple-element.50), channel_id=1, source_target_pairs={{0,8},{8,9},{9,1},{1,2},{2,10},{10,11},{11,3},{3,4},{4,12},{12,13}... | collective-permute-start | bytes 1474568 | tf_op jit(solution)/shard_map/ppermute | solution.py:526
  60.8 8.7 %collective-permute-done.3.lr.fr = f32[5,8,24,128]{3,2,1,0:T(8,128)S(1)} collective-permute-done((f32[5,8,24,128]{3,2,1,0:T(8,128)S(1)}, f32[5,8,24,128]{3,2,1,0:T(8,128)S(1)}, u32[]{:S(2)}, u32[]{:S(2)}) %collective-permute-start.3) | collective-permute-done | bytes 491552 | tf_op jit(solution)/shard_map/ppermute | solution.py:526
  69.5 0.0 collective-permute-done.2.ll.fl
  69.5 12.0 %middle.1 = (f32[16,256,128]{2,1,0:T(8,128)}, f32[32,80,128]{2,1,0:T(8,128)}, f32[32,80,128]{2,1,0:T(8,128)}, f32[1,8,32,128]{3,2,1,0:T(8,128)S(1)}, f32[8,128]{1,0:T(8,128)S(1)}) custom-call(f32[5,8,32,128]{3,2,1,0:T(8,128)S(1)} %get-tuple-element.29.l1.f1, f32[5,8,24,128]{3,2,1,0:T(8,128)S(1)} %collective-permute-done.2.ll.fl, ...), custom_call_target="tpu_custom_call" | custom-call | flops 1000000 | bytes 1000000 | tf_op jit(solution)/shard_map/middle/pallas_call | solution.py:487
  81.5 0.0 copy-done
  81.5 3.3 %collective-permute-start.5 = (f32[1,8,24,128]{3,2,1,0:T(8,128)S(1)}, f32[1,8,24,128]{3,2,1,0:T(8,128)S(1)}, u32[]{:S(2)}, u32[]{:S(2)}) collective-permute-start(f32[1,8,24,128]{3,2,1,0:T(8,128)S(1)} %get-tuple-element.51), channel_id=1, source_target_pairs={{8,0},{9,8},{1,9},{2,1},{10,2},{11,10},{3,11},{4,3},{12,4},{13,12}... | collective-permute-start | bytes 294920 | tf_op jit(solution)/shard_map/ppermute | solution.py:526
  84.9 2.5 %collective-permute-start.4 = (f32[1,8,24,128]{3,2,1,0:T(8,128)S(1)}, f32[1,8,24,128]{3,2,1,0:T(8,128)S(1)}, u32[]{:S(2)}, u32[]{:S(2)}) collective-permute-start(f32[1,8,24,128]{3,2,1,0:T(8,128)S(1)} %get-tuple-element.52), channel_id=1, source_target_pairs={{0,8},{8,9},{9,1},{1,2},{2,10},{10,11},{11,3},{3,4},{4,12},{12,13}... | collective-permute-start | bytes 294920 | tf_op jit(solution)/shard_map/ppermute | solution.py:526
  87.4 0.7 collective-permute-done.5.fr
  88.1 2.7 %collective-permute-done.4.fl = f32[1,8,24,128]{3,2,1,0:T(8,128)S(1)} collective-permute-done((f32[1,8,24,128]{3,2,1,0:T(8,128)S(1)}, f32[1,8,24,128]{3,2,1,0:T(8,128)S(1)}, u32[]{:S(2)}, u32[]{:S(2)}) %collective-permute-start.4) | collective-permute-done | bytes 98336 | tf_op jit(solution)/shard_map/ppermute | solution.py:526
  90.8 0.6 copy-done.3
  91.4 3.9 %all-to-all-start.1 = ((f32[16,256,128]{2,1,0:T(8,128)}), f32[16,256,128]{2,1,0:T(8,128)S(1)}, u32[]{:S(2)}, u32[]{:S(2)}) async-start(f32[16,256,128]{2,1,0:T(8,128)} %get-tuple-element.45), calls=%async_computation.1 | async-start | bytes 4194304 | tf_op jit(solution)/shard_map/all_to_all | solution.py:574
  95.3 0.0 copy-start.1
  95.4 1.0 copy-done.1
  96.4 0.9 copy-done.4
  97.3 7.7 %last.1 = (f32[16,136,128]{2,1,0:T(8,128)}, f32[8,128]{1,0:T(8,128)S(1)}) custom-call(s32[1]{0:T(128)} %bitcast.1.lab_ref, f32[5,8,32,128]{3,2,1,0:T(8,128)S(1)} %get-tuple-element.29.l1.f1, f32[5,8,24,128]{3,2,1,0:T(8,128)S(1)} %copy-done.1, f32[5,8,24,128]{3,2,1,0:T(8,128)S(1)} %collective-permute-done.3.lr.fr, ...), custom_call_target="tpu_custom_call" | custom-call | flops 1000000 | bytes 1000000 | tf_op jit(solution)/shard_map/last/pallas_call | solution.py:487
  105.0 0.0 copy-start.2
  105.0 10.7 %psum.7 = f32[8,128]{1,0:T(8,128)S(1)} all-reduce(f32[8,128]{1,0:T(8,128)S(1)} %get-tuple-element.47), channel_id=1, replica_groups=mesh['gx'=4,'gy'=4,'gz'=8] {'gz'}, use_global_device_ids=true, to_apply=%region_0.1 | all-reduce | flops 1024 | bytes 8192 | tf_op jit(solution)/shard_map/psum | solution.py:585
  115.8 11.0 %all-to-all-done.1.zq_ref = f32[16,256,128]{2,1,0:T(8,128)S(1)} async-done(((f32[16,256,128]{2,1,0:T(8,128)}), f32[16,256,128]{2,1,0:T(8,128)S(1)}, u32[]{:S(2)}, u32[]{:S(2)}) %all-to-all-start.1) | async-done | bytes 2097184 | tf_op jit(solution)/shard_map/all_to_all | solution.py:574
  126.8 0.6 broadcast_dynamic-update-slice_fusion
  127.4 21.0 %all_to_all.16.sums_ref.w_ref = f32[16,136,128]{2,1,0:T(8,128)S(1)} all-to-all(f32[16,136,128]{2,1,0:T(8,128)} %broadcast_dynamic-update-slice_fusion), channel_id=1, replica_groups=mesh['gx'=4,'gy'=4,'gz'=8] {'gx','gy'}, dimensions={0} | all-to-all | bytes 2228224 | tf_op jit(solution)/shard_map/all_to_all | solution.py:588
  148.4 0.0 copy-done.2
  148.4 2.6 %output.1 = (f32[8,8,32,128]{3,2,1,0:T(8,128)}, f32[8,8,32,128]{3,2,1,0:T(8,128)}, f32[8,8,32,128]{3,2,1,0:T(8,128)}) custom-call(s32[1]{0:T(128)} %bitcast.odd_ref, s32[8,32,128]{2,1,0:T(8,128)S(1)} %copy-done.2, f32[16,136,128]{2,1,0:T(8,128)S(1)} %all_to_all.16.sums_ref.w_ref, f32[16,256,128]{2,1,0:T(8,128)S(1)} %all-to-all-done.1.zq_ref, ...), custom_call_target="tpu_custom_call" | custom-call | tf_op jit(solution)/shard_map/output/pallas_call | solution.py:591
  (4 shorter events, 0.0 us)
Async XLA Ops:
  38.7 7.7 %collective-permute-start = (f32[64,8,128]{2,1,0:T(8,128)S(1)}, f32[64,8,128]{2,1,0:T(8,128)S(1)}, u32[]{:S(2)}, u32[]{:S(2)}) collective-permute-start(f32[64,8,128]{2,1,0:T(8,128)S(1)} %get-tuple-element.27), channel_id=1, source_target_pairs={{0,8},{8,9},{9,1},{1,2},{2,10},{10,11},{11,3},{3,4},{4,12},{12,13}... | collective-permute-start | bytes 786440 | tf_op jit(solution)/shard_map/ppermute | solution.py:526
  41.2 8.3 %collective-permute-start.1 = (f32[64,8,128]{2,1,0:T(8,128)S(1)}, f32[64,8,128]{2,1,0:T(8,128)S(1)}, u32[]{:S(2)}, u32[]{:S(2)}) collective-permute-start(f32[64,8,128]{2,1,0:T(8,128)S(1)} %get-tuple-element.28), channel_id=1, source_target_pairs={{8,0},{9,8},{1,9},{2,1},{10,2},{11,10},{3,11},{4,3},{12,4},{13,12}... | collective-permute-start | bytes 786440 | tf_op jit(solution)/shard_map/ppermute | solution.py:526
  54.9 14.6 %collective-permute-start.3 = (f32[5,8,24,128]{3,2,1,0:T(8,128)S(1)}, f32[5,8,24,128]{3,2,1,0:T(8,128)S(1)}, u32[]{:S(2)}, u32[]{:S(2)}) collective-permute-start(f32[5,8,24,128]{3,2,1,0:T(8,128)S(1)} %get-tuple-element.49), channel_id=1, source_target_pairs={{8,0},{9,8},{1,9},{2,1},{10,2},{11,10},{3,11},{4,3},{12,4},{13,12}... | collective-permute-start | bytes 1474568 | tf_op jit(solution)/shard_map/ppermute | solution.py:526
  57.5 12.0 %collective-permute-start.2 = (f32[5,8,24,128]{3,2,1,0:T(8,128)S(1)}, f32[5,8,24,128]{3,2,1,0:T(8,128)S(1)}, u32[]{:S(2)}, u32[]{:S(2)}) collective-permute-start(f32[5,8,24,128]{3,2,1,0:T(8,128)S(1)} %get-tuple-element.50), channel_id=1, source_target_pairs={{0,8},{8,9},{9,1},{1,2},{2,10},{10,11},{11,3},{3,4},{4,12},{12,13}... | collective-permute-start | bytes 1474568 | tf_op jit(solution)/shard_map/ppermute | solution.py:526
  69.5 12.0 %copy-start = (f32[5,8,24,128]{3,2,1,0:T(8,128)}, f32[5,8,24,128]{3,2,1,0:T(8,128)S(1)}, u32[]{:S(2)}) copy-start(f32[5,8,24,128]{3,2,1,0:T(8,128)S(1)} %collective-permute-done.2.ll.fl) | copy-start | bytes 1474564
  81.5 6.5 %collective-permute-start.5 = (f32[1,8,24,128]{3,2,1,0:T(8,128)S(1)}, f32[1,8,24,128]{3,2,1,0:T(8,128)S(1)}, u32[]{:S(2)}, u32[]{:S(2)}) collective-permute-start(f32[1,8,24,128]{3,2,1,0:T(8,128)S(1)} %get-tuple-element.51), channel_id=1, source_target_pairs={{8,0},{9,8},{1,9},{2,1},{10,2},{11,10},{3,11},{4,3},{12,4},{13,12}... | collective-permute-start | bytes 294920 | tf_op jit(solution)/shard_map/ppermute | solution.py:526
  84.9 5.9 %collective-permute-start.4 = (f32[1,8,24,128]{3,2,1,0:T(8,128)S(1)}, f32[1,8,24,128]{3,2,1,0:T(8,128)S(1)}, u32[]{:S(2)}, u32[]{:S(2)}) collective-permute-start(f32[1,8,24,128]{3,2,1,0:T(8,128)S(1)} %get-tuple-element.52), channel_id=1, source_target_pairs={{0,8},{8,9},{9,1},{1,2},{2,10},{10,11},{11,3},{3,4},{4,12},{12,13}... | collective-permute-start | bytes 294920 | tf_op jit(solution)/shard_map/ppermute | solution.py:526
  90.8 0.6 copy-start.3
  91.4 35.3 %all-to-all-start.1 = ((f32[16,256,128]{2,1,0:T(8,128)}), f32[16,256,128]{2,1,0:T(8,128)S(1)}, u32[]{:S(2)}, u32[]{:S(2)}) async-start(f32[16,256,128]{2,1,0:T(8,128)} %get-tuple-element.45), calls=%async_computation.1 | async-start | bytes 4194304 | tf_op jit(solution)/shard_map/all_to_all | solution.py:574
  95.3 1.0 copy-start.1
  96.4 0.9 copy-start.4
  105.0 43.4 %copy-start.2 = (s32[8,32,128]{2,1,0:T(8,128)S(1)}, s32[8,32,128]{2,1,0:T(8,128)}, u32[]{:S(2)}) copy-start(s32[8,32,128]{2,1,0:T(8,128)} %seed_ref.1) | copy-start | bytes 393220

commit v4 on v3

--- a/solution.py
+++ b/solution.py
@@ -205,7 +205,7 @@
         uy_ref[x] = jnp.where(lane == 127, 0.0, edge_weight(lanes(v, -1) - v))
         uz_ref[x] = jnp.where(cut, 0.0, edge_weight(rows(v, -1) - v))
 
-    loop(32, body, 4)
+    loop(32, body)
     even = lane_id((32, 128)) % 2 == 0
 
     def coarse(x):

time: 152 us -> 152 us (level)
  no operation moved by 1% of the time
where the time goes in v4:
time: 152 us; the launch traced here: 151 us
  blocking collectives  68 us (45%)
  Pallas kernels  29.5 us (19%)
  waiting for transfers between devices  28.2 us (19%)
  starting transfers between devices  21.2 us (14%)
  local copies, waits for them, and re-layouts  3.29 us (2%)
    all_to_all x1, blocking collectives, local(): got = lax.all_to_all(sent, group, 0, 0, tiled=True)  36.2 us
    pallas_call x5, Pallas kernels, call(): pl.pallas_call(kernel, out_shape=[pltpu.HBM(shape, F32) if far else sds(*...  26.9 us
    all_to_all x1, blocking collectives, local(): wr_ = lax.all_to_all(wo, group, 0, 0, tiled=True)  21 us
    ppermute x6, starting transfers between devices, swap(): return (lax.ppermute(last, every, up), lax.ppermute(first, every, down))  17.2 us
    ppermute x6, waiting for transfers between devices, swap(): return (lax.ppermute(last, every, up), lax.ppermute(first, every, down))  17.2 us
    all_to_all x1, waiting for transfers between devices, local(): zqr = lax.all_to_all(zq, group, 0, 0, tiled=True)  11 us
    psum x1, blocking collectives, local(): sums = lax.psum(line, 'gz')  10.7 us
    all_to_all x1, starting transfers between devices, local(): zqr = lax.all_to_all(zq, group, 0, 0, tiled=True)  3.91 us
  transfers between devices with their start and end apart: 7, of which 6 were waited for; matrix products, arithmetic and copies ran while one was open for 0% of the time, Pallas kernels for 5%

profile of v4, /device:TPU:4, one launch (start us, length us, event | category | flops | bytes accessed | tf_op | source)
XLA Modules:
  0.0 151.0 jit_solution(15434370483918418623)
XLA Ops:
  0.6 1.2 pack.1
  1.9 36.2 %all_to_all.15.r_ref = f32[16,8,32,128]{3,2,1,0:T(8,128)S(1)} all-to-all(f32[16,8,32,128]{3,2,1,0:T(8,128)S(1)} %pack.1), channel_id=1, replica_groups=mesh['gx'=4,'gy'=4,'gz'=8] {'gx','gy'}, dimensions={0} | all-to-all | bytes 4194304 | tf_op jit(solution)/shard_map/all_to_all | solution.py:545
  38.1 0.6 turn.1
  38.7 2.5 %collective-permute-start = (f32[64,8,128]{2,1,0:T(8,128)S(1)}, f32[64,8,128]{2,1,0:T(8,128)S(1)}, u32[]{:S(2)}, u32[]{:S(2)}) collective-permute-start(f32[64,8,128]{2,1,0:T(8,128)S(1)} %get-tuple-element.27), channel_id=1, source_target_pairs={{0,8},{8,9},{9,1},{1,2},{2,10},{10,11},{11,3},{3,4},{4,12},{12,13}... | collective-permute-start | bytes 786440 | tf_op jit(solution)/shard_map/ppermute | solution.py:526
  41.2 3.1 %collective-permute-start.1 = (f32[64,8,128]{2,1,0:T(8,128)S(1)}, f32[64,8,128]{2,1,0:T(8,128)S(1)}, u32[]{:S(2)}, u32[]{:S(2)}) collective-permute-start(f32[64,8,128]{2,1,0:T(8,128)S(1)} %get-tuple-element.28), channel_id=1, source_target_pairs={{8,0},{9,8},{1,9},{2,1},{10,2},{11,10},{3,11},{4,3},{12,4},{13,12}... | collective-permute-start | bytes 786440 | tf_op jit(solution)/shard_map/ppermute | solution.py:526
  44.3 2.1 %collective-permute-done.left_hbm = f32[64,8,128]{2,1,0:T(8,128)S(1)} collective-permute-done((f32[64,8,128]{2,1,0:T(8,128)S(1)}, f32[64,8,128]{2,1,0:T(8,128)S(1)}, u32[]{:S(2)}, u32[]{:S(2)}) %collective-permute-start) | collective-permute-done | bytes 262176 | tf_op jit(solution)/shard_map/ppermute | solution.py:526
  46.4 3.1 %collective-permute-done.1.right_hbm = f32[64,8,128]{2,1,0:T(8,128)S(1)} collective-permute-done((f32[64,8,128]{2,1,0:T(8,128)S(1)}, f32[64,8,128]{2,1,0:T(8,128)S(1)}, u32[]{:S(2)}, u32[]{:S(2)}) %collective-permute-start.1) | collective-permute-done | bytes 262176 | tf_op jit(solution)/shard_map/ppermute | solution.py:526
  49.5 5.3 %first.1 = (f32[33,80,128]{2,1,0:T(8,128)}, f32[32,80,128]{2,1,0:T(8,128)}, f32[32,80,128]{2,1,0:T(8,128)}, f32[32,80,128]{2,1,0:T(8,128)}, f32[32,80,128]{2,1,0...) custom-call(s32[1]{0:T(128)} %bitcast.2.zb_ref, s32[1]{0:T(128)} %bitcast.1.lab_ref, ...), custom_call_target="tpu_custom_call" | custom-call | flops 1000000 | bytes 1000000 | tf_op jit(solution)/shard_map/first/pallas_call | solution.py:487
  54.8 0.1 fusion
  54.9 2.5 %collective-permute-start.3 = (f32[5,8,24,128]{3,2,1,0:T(8,128)S(1)}, f32[5,8,24,128]{3,2,1,0:T(8,128)S(1)}, u32[]{:S(2)}, u32[]{:S(2)}) collective-permute-start(f32[5,8,24,128]{3,2,1,0:T(8,128)S(1)} %get-tuple-element.49), channel_id=1, source_target_pairs={{8,0},{9,8},{1,9},{2,1},{10,2},{11,10},{3,11},{4,3},{12,4},{13,12}... | collective-permute-start | bytes 1474568 | tf_op jit(solution)/shard_map/ppermute | solution.py:526
  57.4 3.3 %collective-permute-start.2 = (f32[5,8,24,128]{3,2,1,0:T(8,128)S(1)}, f32[5,8,24,128]{3,2,1,0:T(8,128)S(1)}, u32[]{:S(2)}, u32[]{:S(2)}) collective-permute-start(f32[5,8,24,128]{3,2,1,0:T(8,128)S(1)} %get-tuple-element.50), channel_id=1, source_target_pairs={{0,8},{8,9},{9,1},{1,2},{2,10},{10,11},{11,3},{3,4},{4,12},{12,13}... | collective-permute-start | bytes 1474568 | tf_op jit(solution)/shard_map/ppermute | solution.py:526
  60.7 8.7 %collective-permute-done.3.lr.fr = f32[5,8,24,128]{3,2,1,0:T(8,128)S(1)} collective-permute-done((f32[5,8,24,128]{3,2,1,0:T(8,128)S(1)}, f32[5,8,24,128]{3,2,1,0:T(8,128)S(1)}, u32[]{:S(2)}, u32[]{:S(2)}) %collective-permute-start.3) | collective-permute-done | bytes 491552 | tf_op jit(solution)/shard_map/ppermute | solution.py:526
  69.4 0.0 collective-permute-done.2.ll.fl
  69.4 12.0 %middle.1 = (f32[16,256,128]{2,1,0:T(8,128)}, f32[32,80,128]{2,1,0:T(8,128)}, f32[32,80,128]{2,1,0:T(8,128)}, f32[1,8,32,128]{3,2,1,0:T(8,128)S(1)}, f32[8,128]{1,0:T(8,128)S(1)}) custom-call(f32[5,8,32,128]{3,2,1,0:T(8,128)S(1)} %get-tuple-element.29.l1.f1, f32[5,8,24,128]{3,2,1,0:T(8,128)S(1)} %collective-permute-done.2.ll.fl, ...), custom_call_target="tpu_custom_call" | custom-call | flops 1000000 | bytes 1000000 | tf_op jit(solution)/shard_map/middle/pallas_call | solution.py:487
  81.5 0.0 copy-done
  81.5 3.3 %collective-permute-start.5 = (f32[1,8,24,128]{3,2,1,0:T(8,128)S(1)}, f32[1,8,24,128]{3,2,1,0:T(8,128)S(1)}, u32[]{:S(2)}, u32[]{:S(2)}) collective-permute-start(f32[1,8,24,128]{3,2,1,0:T(8,128)S(1)} %get-tuple-element.51), channel_id=1, source_target_pairs={{8,0},{9,8},{1,9},{2,1},{10,2},{11,10},{3,11},{4,3},{12,4},{13,12}... | collective-permute-start | bytes 294920 | tf_op jit(solution)/shard_map/ppermute | solution.py:526
  84.8 2.5 %collective-permute-start.4 = (f32[1,8,24,128]{3,2,1,0:T(8,128)S(1)}, f32[1,8,24,128]{3,2,1,0:T(8,128)S(1)}, u32[]{:S(2)}, u32[]{:S(2)}) collective-permute-start(f32[1,8,24,128]{3,2,1,0:T(8,128)S(1)} %get-tuple-element.52), channel_id=1, source_target_pairs={{0,8},{8,9},{9,1},{1,2},{2,10},{10,11},{11,3},{3,4},{4,12},{12,13}... | collective-permute-start | bytes 294920 | tf_op jit(solution)/shard_map/ppermute | solution.py:526
  87.4 0.7 collective-permute-done.5.fr
  88.0 2.7 %collective-permute-done.4.fl = f32[1,8,24,128]{3,2,1,0:T(8,128)S(1)} collective-permute-done((f32[1,8,24,128]{3,2,1,0:T(8,128)S(1)}, f32[1,8,24,128]{3,2,1,0:T(8,128)S(1)}, u32[]{:S(2)}, u32[]{:S(2)}) %collective-permute-start.4) | collective-permute-done | bytes 98336 | tf_op jit(solution)/shard_map/ppermute | solution.py:526
  90.7 0.6 copy-done.3
  91.4 3.9 %all-to-all-start.1 = ((f32[16,256,128]{2,1,0:T(8,128)}), f32[16,256,128]{2,1,0:T(8,128)S(1)}, u32[]{:S(2)}, u32[]{:S(2)}) async-start(f32[16,256,128]{2,1,0:T(8,128)} %get-tuple-element.45), calls=%async_computation.1 | async-start | bytes 4194304 | tf_op jit(solution)/shard_map/all_to_all | solution.py:574
  95.3 0.0 copy-start.1
  95.3 1.0 copy-done.1
  96.3 0.9 copy-done.4
  97.2 7.7 %last.1 = (f32[16,136,128]{2,1,0:T(8,128)}, f32[8,128]{1,0:T(8,128)S(1)}) custom-call(s32[1]{0:T(128)} %bitcast.1.lab_ref, f32[5,8,32,128]{3,2,1,0:T(8,128)S(1)} %get-tuple-element.29.l1.f1, f32[5,8,24,128]{3,2,1,0:T(8,128)S(1)} %copy-done.1, f32[5,8,24,128]{3,2,1,0:T(8,128)S(1)} %collective-permute-done.3.lr.fr, ...), custom_call_target="tpu_custom_call" | custom-call | flops 1000000 | bytes 1000000 | tf_op jit(solution)/shard_map/last/pallas_call | solution.py:487
  105.0 0.0 copy-start.2
  105.0 10.7 %psum.7 = f32[8,128]{1,0:T(8,128)S(1)} all-reduce(f32[8,128]{1,0:T(8,128)S(1)} %get-tuple-element.47), channel_id=1, replica_groups=mesh['gx'=4,'gy'=4,'gz'=8] {'gz'}, use_global_device_ids=true, to_apply=%region_0.1 | all-reduce | flops 1024 | bytes 8192 | tf_op jit(solution)/shard_map/psum | solution.py:585
  115.7 11.0 %all-to-all-done.1.zq_ref = f32[16,256,128]{2,1,0:T(8,128)S(1)} async-done(((f32[16,256,128]{2,1,0:T(8,128)}), f32[16,256,128]{2,1,0:T(8,128)S(1)}, u32[]{:S(2)}, u32[]{:S(2)}) %all-to-all-start.1) | async-done | bytes 2097184 | tf_op jit(solution)/shard_map/all_to_all | solution.py:574
  126.7 0.6 broadcast_dynamic-update-slice_fusion
  127.3 21.0 %all_to_all.16.sums_ref.w_ref = f32[16,136,128]{2,1,0:T(8,128)S(1)} all-to-all(f32[16,136,128]{2,1,0:T(8,128)} %broadcast_dynamic-update-slice_fusion), channel_id=1, replica_groups=mesh['gx'=4,'gy'=4,'gz'=8] {'gx','gy'}, dimensions={0} | all-to-all | bytes 2228224 | tf_op jit(solution)/shard_map/all_to_all | solution.py:588
  148.4 0.0 copy-done.2
  148.4 2.6 %output.1 = (f32[8,8,32,128]{3,2,1,0:T(8,128)}, f32[8,8,32,128]{3,2,1,0:T(8,128)}, f32[8,8,32,128]{3,2,1,0:T(8,128)}) custom-call(s32[1]{0:T(128)} %bitcast.odd_ref, s32[8,32,128]{2,1,0:T(8,128)S(1)} %copy-done.2, f32[16,136,128]{2,1,0:T(8,128)S(1)} %all_to_all.16.sums_ref.w_ref, f32[16,256,128]{2,1,0:T(8,128)S(1)} %all-to-all-done.1.zq_ref, ...), custom_call_target="tpu_custom_call" | custom-call | tf_op jit(solution)/shard_map/output/pallas_call | solution.py:591
  (4 shorter events, 0.0 us)
Async XLA Ops:
  38.7 7.7 %collective-permute-start = (f32[64,8,128]{2,1,0:T(8,128)S(1)}, f32[64,8,128]{2,1,0:T(8,128)S(1)}, u32[]{:S(2)}, u32[]{:S(2)}) collective-permute-start(f32[64,8,128]{2,1,0:T(8,128)S(1)} %get-tuple-element.27), channel_id=1, source_target_pairs={{0,8},{8,9},{9,1},{1,2},{2,10},{10,11},{11,3},{3,4},{4,12},{12,13}... | collective-permute-start | bytes 786440 | tf_op jit(solution)/shard_map/ppermute | solution.py:526
  41.2 8.3 %collective-permute-start.1 = (f32[64,8,128]{2,1,0:T(8,128)S(1)}, f32[64,8,128]{2,1,0:T(8,128)S(1)}, u32[]{:S(2)}, u32[]{:S(2)}) collective-permute-start(f32[64,8,128]{2,1,0:T(8,128)S(1)} %get-tuple-element.28), channel_id=1, source_target_pairs={{8,0},{9,8},{1,9},{2,1},{10,2},{11,10},{3,11},{4,3},{12,4},{13,12}... | collective-permute-start | bytes 786440 | tf_op jit(solution)/shard_map/ppermute | solution.py:526
  54.9 14.6 %collective-permute-start.3 = (f32[5,8,24,128]{3,2,1,0:T(8,128)S(1)}, f32[5,8,24,128]{3,2,1,0:T(8,128)S(1)}, u32[]{:S(2)}, u32[]{:S(2)}) collective-permute-start(f32[5,8,24,128]{3,2,1,0:T(8,128)S(1)} %get-tuple-element.49), channel_id=1, source_target_pairs={{8,0},{9,8},{1,9},{2,1},{10,2},{11,10},{3,11},{4,3},{12,4},{13,12}... | collective-permute-start | bytes 1474568 | tf_op jit(solution)/shard_map/ppermute | solution.py:526
  57.4 12.0 %collective-permute-start.2 = (f32[5,8,24,128]{3,2,1,0:T(8,128)S(1)}, f32[5,8,24,128]{3,2,1,0:T(8,128)S(1)}, u32[]{:S(2)}, u32[]{:S(2)}) collective-permute-start(f32[5,8,24,128]{3,2,1,0:T(8,128)S(1)} %get-tuple-element.50), channel_id=1, source_target_pairs={{0,8},{8,9},{9,1},{1,2},{2,10},{10,11},{11,3},{3,4},{4,12},{12,13}... | collective-permute-start | bytes 1474568 | tf_op jit(solution)/shard_map/ppermute | solution.py:526
  69.4 12.0 %copy-start = (f32[5,8,24,128]{3,2,1,0:T(8,128)}, f32[5,8,24,128]{3,2,1,0:T(8,128)S(1)}, u32[]{:S(2)}) copy-start(f32[5,8,24,128]{3,2,1,0:T(8,128)S(1)} %collective-permute-done.2.ll.fl) | copy-start | bytes 1474564
  81.5 6.5 %collective-permute-start.5 = (f32[1,8,24,128]{3,2,1,0:T(8,128)S(1)}, f32[1,8,24,128]{3,2,1,0:T(8,128)S(1)}, u32[]{:S(2)}, u32[]{:S(2)}) collective-permute-start(f32[1,8,24,128]{3,2,1,0:T(8,128)S(1)} %get-tuple-element.51), channel_id=1, source_target_pairs={{8,0},{9,8},{1,9},{2,1},{10,2},{11,10},{3,11},{4,3},{12,4},{13,12}... | collective-permute-start | bytes 294920 | tf_op jit(solution)/shard_map/ppermute | solution.py:526
  84.8 5.9 %collective-permute-start.4 = (f32[1,8,24,128]{3,2,1,0:T(8,128)S(1)}, f32[1,8,24,128]{3,2,1,0:T(8,128)S(1)}, u32[]{:S(2)}, u32[]{:S(2)}) collective-permute-start(f32[1,8,24,128]{3,2,1,0:T(8,128)S(1)} %get-tuple-element.52), channel_id=1, source_target_pairs={{0,8},{8,9},{9,1},{1,2},{2,10},{10,11},{11,3},{3,4},{4,12},{12,13}... | collective-permute-start | bytes 294920 | tf_op jit(solution)/shard_map/ppermute | solution.py:526
  90.7 0.6 copy-start.3
  91.4 35.3 %all-to-all-start.1 = ((f32[16,256,128]{2,1,0:T(8,128)}), f32[16,256,128]{2,1,0:T(8,128)S(1)}, u32[]{:S(2)}, u32[]{:S(2)}) async-start(f32[16,256,128]{2,1,0:T(8,128)} %get-tuple-element.45), calls=%async_computation.1 | async-start | bytes 4194304 | tf_op jit(solution)/shard_map/all_to_all | solution.py:574
  95.3 1.0 copy-start.1
  96.3 0.9 copy-start.4
  105.0 43.4 %copy-start.2 = (s32[8,32,128]{2,1,0:T(8,128)S(1)}, s32[8,32,128]{2,1,0:T(8,128)}, u32[]{:S(2)}) copy-start(s32[8,32,128]{2,1,0:T(8,128)} %seed_ref.1) | copy-start | bytes 393220
